TPU v7x, 256 devices: a whole 4x4x8 slice. The times are simulated.
256 devices in a mesh: cell: 64 (over z_hi, y, x), orb: 4 (over z_lo, core).
Axes of the slice: x: 4, y: 4, z: 8 (z_hi: 4, z_lo: 2; z = z_hi * 2 + z_lo), core: 2. Of those that a mesh axis runs over, the one named last changes fastest.
Arguments:
- orbitals: bfloat16 [256, 663552], P('orb', 'cell'), may hold values from -6 to 6
- panels: bfloat16 [128, 663552], P('orb', 'cell'), may hold values from -0.01953125 to 0.01953125
- stiffness: bfloat16 [343, 343], replicated, may hold values from -0.3 to 2.5
- potential: float32 [343, 3072], P(None, 'cell'), may hold values from -1 to 3
- connectivity: int32 [343, 3072], P(None, 'cell'), may hold values from 0 to 12095, as said below
- boundary: int32 [110592], P('cell'), may hold values from 0 to 10367, as said below
Outputs:
- applied: bfloat16 [256, 663552], P('orb', 'cell')
- projected: float32 [128, 256], P('cell', 'orb')
Inputs may be any that keep to these rules, and one draw needn't show every extreme that they name: `connectivity`: A partition's entries number its own 10368 nodes below 10368 and, from 10368 on, the 1728 nodes it shares with the next partition, in the order of that partition's boundary entries; every number is used by some cell. `boundary`: A partition's 1728 entries are distinct numbers of its own nodes.
All inputs are finite; a program needn't handle non-finite values.
Results may differ from a plain program's by a relative error of at most 0.0028.
Values may be sent and summed in bfloat16 or wider, within the bound.
A program may use at most 64 MiB of HBM per device.

v0:
```python
import jax
import jax.numpy as jnp
from jax import lax
from jax.sharding import PartitionSpec as P


def shifted(block, axis, distance):
    devices = range(lax.axis_size(axis))
    route = [(i - distance, i) for i in devices if i - distance in devices]
    return lax.ppermute(block, axis, route)


def shards(orbitals, panels, stiffness, potential, connectivity, boundary):
    own_count = orbitals.shape[1]
    edge_values = jnp.take(orbitals, boundary, axis=1)
    ghost_vals = shifted(edge_values, "cell", -1)
    local = jnp.concatenate([orbitals, ghost_vals], axis=1)
    gathered = jnp.take(local, connectivity, axis=1)
    element_out = jnp.einsum("ij,bjc->bic", stiffness, gathered, preferred_element_type=jnp.float32)
    element_out = element_out + potential[None] * gathered.astype(jnp.float32)
    assembled = (
        jnp.zeros((orbitals.shape[0], local.shape[1]), jnp.float32)
        .at[:, connectivity]
        .add(element_out)
    )
    incoming = shifted(assembled[:, own_count:], "cell", 1)
    owned = assembled[:, :own_count].at[:, boundary].add(incoming)
    applied = owned.astype(jnp.bfloat16)
    term = lax.dot_general(
        lax.all_gather(panels, "orb", axis=0, tiled=True),
        applied,
        (((1,), (1,)), ((), ())),
        preferred_element_type=jnp.float32,
    )
    projected = lax.psum_scatter(term, "cell", scatter_dimension=0, tiled=True)
    return (applied, projected)


def solution(mesh):
    return jax.shard_map(
        shards,
        mesh=mesh,
        in_specs=(
            P("orb", "cell"),
            P("orb", "cell"),
            P(),
            P(None, "cell"),
            P(None, "cell"),
            P("cell"),
        ),
        out_specs=(P("orb", "cell"), P("cell", "orb")),
        check_vma=False,
    )
```

profile of v0, /device:TPU:160, one launch (start us, length us, event | category | flops | bytes accessed | tf_op | source)
XLA Modules:
  0.0 625.6 jit_solution(13283267120086458746)
XLA Ops:
  7.2 0.7 all-gather.2.cloned.1.call-update
  7.9 0.7 compare_select_fusion.1
  8.6 2.9 copy.23
  11.6 3.9 gather_fusion
  15.5 1.1 select_bitcast_fusion
  16.6 7.1 %collective-permute-start = (bf16[64,1728]{0,1:T(8,128)(2,1)}, bf16[64,1728]{0,1:T(8,128)(2,1)}, u32[]{:S(2)}, u32[]{:S(2)}) collective-permute-start(bf16[64,1728]{0,1:T(8,128)(2,1)} %select_bitcast_fusion), channel_id=1, source_target_pairs={{4,0},{8,4},{12,8},{16,12},{20,16},{24,20},{28,24},{32,28},{36,32}... | collective-permute-start | bytes 663560 | tf_op jit(solution)/shard_map/ppermute | solution.py:10
  24.6 28.0 %collective-permute-done = bf16[64,1728]{0,1:T(8,128)(2,1)} collective-permute-done((bf16[64,1728]{0,1:T(8,128)(2,1)}, bf16[64,1728]{0,1:T(8,128)(2,1)}, u32[]{:S(2)}, u32[]{:S(2)}) %collective-permute-start) | collective-permute-done | bytes 221216 | tf_op jit(solution)/shard_map/ppermute | solution.py:10
  52.6 3.4 pad_maximum_fusion
  56.0 33.9 %gather_fusion.1 = bf16[16464,64]{1,0:T(8,128)(2,1)} fusion(bf16[64,12096]{0,1:T(8,128)(2,1)S(1)} %pad_maximum_fusion, s32[17408]{0:T(1024)S(1)} %pad_clamp_fusion), kind=kCustom, calls=%fused_computation.1 | custom fusion | bytes 4280640 | tf_op jit(solution)/shard_map/jit(_take)/gather | solution.py:18
  90.0 5.6 copy.25
  95.5 4.1 fusion
  99.6 8.0 %copy.34 = f32[343,48,64]{2,1,0:T(8,128)} copy(f32[343,48,64]{0,1,2:T(8,128)} %fusion) | data formatting | bytes 8429568 | tf_op jit(solution)/shard_map/add | solution.py:20
  107.6 93.7 %scatter_custom_fusion = f32[64,12096]{0,1:T(8,128)} fusion(s32[16464]{0:T(1024)} %copy-done.3, f32[16464,64]{1,0:T(8,128)} %bitcast.28, f32[]{:T(128)} %constant.18.clone.1), kind=kCustom, calls=%fused_computation.7 | custom fusion | flops 1053696 | bytes 3097088 | tf_op jit(solution)/shard_map/scatter-add | solution.py:24
  201.3 1.2 slice.13
  202.8 2.1 collective-permute-start.1
  205.0 0.6 dynamic-slice
  206.2 4.3 slice.12
  210.5 12.1 %collective-permute-done.1 = f32[64,1728]{1,0:T(8,128)S(1)} collective-permute-done((f32[64,1728]{1,0:T(8,128)S(1)}, f32[64,1728]{1,0:T(8,128)S(1)}, u32[]{:S(2)}, u32[]{:S(2)}) %collective-permute-start.1) | collective-permute-done | bytes 442400 | tf_op jit(solution)/shard_map/ppermute | solution.py:10
  222.8 15.3 %scatter_fusion = f32[64,10368]{0,1:T(8,128)} fusion(f32[64,10368]{0,1:T(8,128)} %slice.12, s32[1728]{0:T(1024)S(1)} %compare_select_fusion.1, f32[1728,64]{1,0:T(8,128)S(1)} %copy.29), kind=kCustom, calls=%fused_computation.3 | custom fusion | flops 110592 | bytes 1334016 | tf_op jit(solution)/shard_map/scatter-add | solution.py:27
  238.1 2.7 convert_element_type.7
  240.9 2.2 copy.30
  243.1 2.9 convolution_bitcast_fusion
  246.0 372.0 %all-reduce = f32[128,64]{0,1:T(8,128)S(1)} all-reduce(f32[128,64]{0,1:T(8,128)S(1)} %convolution_bitcast_fusion), channel_id=2, replica_groups=mesh['cell'=64,'orb'=4] {'cell'}, use_global_device_ids=true, to_apply=%region_2.3.clone | all-reduce | flops 8192 | bytes 65536
  618.1 0.6 copy.31
  (26 shorter events, 1.6 us)
Async XLA Ops:
  7.2 88.4 %copy-start = (bf16[343,343]{1,0:T(8,128)(2,1)S(1)}, bf16[343,343]{1,0:T(8,128)(2,1)}, u32[]{:S(2)}) copy-start(bf16[343,343]{1,0:T(8,128)(2,1)} %param.8) | copy-start | bytes 705898
  7.2 8.3 %copy-start.4 = (s32[1728]{0:T(1024)S(1)}, s32[1728]{0:T(1024)}, u32[]{:S(2)}) copy-start(s32[1728]{0:T(1024)} %param.11) | copy-start | bytes 20740
  7.2 16.5 %copy-start.2 = (s32[343,48]{0,1:T(8,128)S(1)}, s32[343,48]{0,1:T(8,128)}, u32[]{:S(2)}) copy-start(s32[343,48]{0,1:T(8,128)} %param.10) | copy-start | bytes 197572
  7.2 235.9 %all-gather.2.cloned.1.call-start = ((), (), s32[]{:S(2)}) async-start(), calls=%async_computation | async-start | bytes 3317760 | tf_op jit(solution)/shard_map/all_gather | solution.py:30
  11.5 12.5 %copy-start.1 = (bf16[64,10368]{0,1:T(8,128)(2,1)}, bf16[64,10368]{0,1:T(8,128)(2,1)S(1)}, u32[]{:S(2)}) copy-start(bf16[64,10368]{0,1:T(8,128)(2,1)S(1)} %copy.23) | copy-start | bytes 3981316
  16.6 36.1 %collective-permute-start = (bf16[64,1728]{0,1:T(8,128)(2,1)}, bf16[64,1728]{0,1:T(8,128)(2,1)}, u32[]{:S(2)}, u32[]{:S(2)}) collective-permute-start(bf16[64,1728]{0,1:T(8,128)(2,1)} %select_bitcast_fusion), channel_id=1, source_target_pairs={{4,0},{8,4},{12,8},{16,12},{20,16},{24,20},{28,24},{32,28},{36,32}... | collective-permute-start | bytes 663560 | tf_op jit(solution)/shard_map/ppermute | solution.py:10
  24.0 0.6 copy-start.3
  90.0 5.6 copy-start.5
  107.6 97.3 %copy-start.6 = (u32[256]{0:T(256)S(1)}, u32[256]{0:T(256)}, u32[]{:S(2)}) copy-start(u32[256]{0:T(256)} %constant.40) | copy-start | bytes 3076
  202.8 19.7 %collective-permute-start.1 = (f32[64,1728]{1,0:T(8,128)S(1)}, f32[64,1728]{1,0:T(8,128)S(1)}, u32[]{:S(2)}, u32[]{:S(2)}) collective-permute-start(f32[64,1728]{1,0:T(8,128)S(1)} %copy.28), channel_id=1, source_target_pairs={{0,4},{4,8},{8,12},{12,16},{16,20},{20,24},{24,28},{28,32},{32,36}... | collective-permute-start | bytes 1327112 | tf_op jit(solution)/shard_map/ppermute | solution.py:10
Sparse Core Ops, SparseCore 0:
  9.8 54.3 all-gather.1
where the time goes:
time: 626 us
  blocking collectives  372 us (59%)
  other arithmetic  117 us (19%)
  local copies, waits for them, and re-layouts  64.7 us (10%)
  waiting for transfers between devices  40.8 us (7%)
  between operations  14.9 us (2%)
  starting transfers between devices  9.23 us (1%)
  matrix products  6.95 us (1%)
    unnamed x1, blocking collectives  372 us
    scatter-add x1, other arithmetic, shards(): assembled = jnp.zeros((orbitals.shape[0], local.shape[1]), jnp.float32).a...  93.7 us
    ppermute x2, waiting for transfers between devices, shifted(): return lax.ppermute(block, axis, route)  40.1 us
    gather x2, local copies, waits for them, and re-layouts, shards(): gathered = jnp.take(local, connectivity, axis=1)  39.5 us
    scatter-add x1, other arithmetic, shards(): owned = assembled[:, :own_count].at[:, boundary].add(incoming)  15.3 us
  transfers between devices with their start and end apart: 3, of which 2 were waited for; matrix products, arithmetic and copies ran while one was open for 29% of the time, Pallas kernels for 0%

commit v1 on v0

v1 whole, which is shorter than its diff:
```python
import jax
import jax.numpy as jnp
from jax import lax
from jax.experimental import pallas as pl
from jax.experimental.pallas import tpu as pltpu
from jax.sharding import PartitionSpec as P

ORB = 64
NPE = 343
ROWS = 344
DEEP = 384
CELLS = 48
HALF_CELLS = 24
OWN = 10368
GHOST = 1728
LOCAL = OWN + GHOST
PANELS = 128
N_CELL = 64
LOW = 5248
HALF_GHOST = 864
PACKED = LOW + HALF_GHOST
BATCH = 8
MIB = 2**20
ANY = pl.BlockSpec(memory_space=pl.ANY)
VMEM = pl.BlockSpec(memory_space=pltpu.VMEM)
SMEM = pl.BlockSpec(memory_space=pltpu.SMEM)
MESH = pl.DeviceIdType.MESH
F32 = jnp.float32
BF16 = jnp.bfloat16


def places():
    cell = lax.axis_index("cell")
    orb = lax.axis_index("orb")
    core = lax.rem(orb, 2)
    peer = {"orb": orb + 1 - 2 * core}
    before = {"cell": lax.rem(cell + N_CELL - 1, N_CELL)}
    after = {"cell": lax.rem(cell + 1, N_CELL)}
    return cell, core, peer, before, after


def greet(signalled, waits):
    barrier = pltpu.get_barrier_semaphore()
    for device in signalled:
        pl.semaphore_signal(barrier, inc=1, device_id=device, device_id_type=MESH)
    pl.semaphore_wait(barrier, waits)


def remote(src, dst, send, recv, device):
    return pltpu.make_async_remote_copy(
        src_ref=src, dst_ref=dst, send_sem=send, recv_sem=recv, device_id=device, device_id_type=MESH
    )


X_CHUNKS = 3
X_WIDE = OWN // X_CHUNKS
G_CHUNKS = 3
G_ROWS = HALF_GHOST // G_CHUNKS


def collect_kernel(
    orb_ref, bound_ref, out_ref, x, table, rows, leaving, landed, local_sem, xs_sem, xr_sem, gs_sem, gr_sem, fs_sem, fr_sem, out_sem
):
    cell, core, peer, before, after = places()
    mine = pl.ds(pl.multiple_of(core * ORB, ORB), ORB)
    columns = [pl.ds(c * X_WIDE, X_WIDE) for c in range(X_CHUNKS)]
    own = [pltpu.make_async_copy(orb_ref.at[:, s], x.at[mine, s], local_sem.at[c]) for c, s in enumerate(columns)]
    for copy in own:
        copy.start()
    greet([peer, after], 2)
    given = [remote(orb_ref.at[:, s], x.at[mine, s], xs_sem.at[c], xr_sem.at[c], peer) for c, s in enumerate(columns)]
    for copy in given:
        copy.start()
    stored = []
    for c in range(X_CHUNKS):
        own[c].wait()
        given[c].wait_recv()

        def turn(b, carry, c=c):
            at = pl.multiple_of(c * X_WIDE + b * 128, 128)
            table[pl.ds(at, 128), :] = x[:, pl.ds(at, 128)].astype(F32).T
            return carry

        lax.fori_loop(0, X_WIDE // 128, turn, 0)
        part = pl.ds(c * X_WIDE, X_WIDE)
        stored.append(pltpu.make_async_copy(table.at[part], out_ref.at[part], out_sem.at[c]))
        stored[-1].start()
    base = core * HALF_GHOST
    sent = []
    for g in range(G_CHUNKS):

        def pick(t, carry, g=g):
            at = g * G_ROWS + t * 16
            for j in range(16):
                rows[pl.ds(j, 1), :] = table[pl.ds(bound_ref[base + at + j], 1), :]
            leaving[pl.ds(pl.multiple_of(at, 16), 16), :] = rows[...].astype(BF16)
            return carry

        lax.fori_loop(0, G_ROWS // 16, pick, 0)
        src = pl.ds(g * G_ROWS, G_ROWS)
        dst = pl.ds(pl.multiple_of(base + g * G_ROWS, 16), G_ROWS)
        sent.append(remote(leaving.at[src], landed.at[dst], gs_sem.at[g], gr_sem.at[g], before))
        sent[-1].start()
    passed = []
    for g in range(G_CHUNKS):
        sent[g].wait_recv()
        dst = pl.ds(pl.multiple_of(base + g * G_ROWS, 16), G_ROWS)
        passed.append(remote(landed.at[dst], landed.at[dst], fs_sem.at[g], fr_sem.at[g], peer))
        passed[-1].start()
    for copy in passed:
        copy.wait_recv()
    inner = cell < N_CELL - 1
    table[OWN:, :] = jnp.where(inner, landed[...].astype(F32), 0.0)
    part = pl.ds(OWN, GHOST)
    stored.append(pltpu.make_async_copy(table.at[part], out_ref.at[part], out_sem.at[X_CHUNKS]))
    stored[-1].start()
    for copy in given + sent + passed:
        copy.wait_send()
    for copy in stored:
        copy.wait()


def collect(orbitals, boundary):
    dma = pltpu.SemaphoreType.DMA
    return pl.pallas_call(
        collect_kernel,
        out_shape=jax.ShapeDtypeStruct((LOCAL, 2 * ORB), F32),
        in_specs=[ANY, SMEM],
        out_specs=ANY,
        scratch_shapes=[
            pltpu.VMEM((2 * ORB, OWN), BF16),
            pltpu.VMEM((LOCAL, 2 * ORB), F32),
            pltpu.VMEM((16, 2 * ORB), F32),
            pltpu.VMEM((HALF_GHOST, 2 * ORB), BF16),
            pltpu.VMEM((GHOST, 2 * ORB), BF16),
            dma((X_CHUNKS,)),
            dma((X_CHUNKS,)),
            dma((X_CHUNKS,)),
            dma((G_CHUNKS,)),
            dma((G_CHUNKS,)),
            dma((G_CHUNKS,)),
            dma((G_CHUNKS,)),
            dma((X_CHUNKS + 1,)),
        ],
        compiler_params=pltpu.CompilerParams(collective_id=0, has_side_effects=True, vmem_limit_bytes=40 * MIB),
    )(orbitals, boundary)


def element_kernel(conn_ref, conn_vec, pot_ref, stiff_ref, table, own_ref, leave_ref, even, odd, gathered, product, weights, scaled):
    core = lax.rem(lax.axis_index("orb"), 2)
    first = core * HALF_CELLS
    even[...] = jnp.zeros_like(even)
    odd[...] = jnp.zeros_like(odd)
    gathered[NPE:, :] = jnp.zeros((DEEP - NPE, 2 * ORB), F32)
    weights[...] = jnp.zeros_like(weights)
    weights[:NPE, :NPE] = stiff_ref[...]
    scaled[...] = jnp.zeros_like(scaled)
    scaled[:NPE, :CELLS] = pot_ref[...]

    alike = jnp.zeros((1, CELLS), jnp.int32)
    for d in range(1, BATCH):
        same = conn_vec[: NPE - d, :] == conn_vec[d:NPE, :]
        alike = jnp.maximum(alike, jnp.max(same.astype(jnp.int32), axis=0, keepdims=True))
    repeats = jnp.max(alike)

    def element(e):
        for j in range(NPE):
            gathered[pl.ds(j, 1), :] = table[pl.ds(conn_ref[j, e], 1), :]
        full = gathered[...]
        level = jnp.take_along_axis(scaled[...], jnp.full((ROWS, 128), e, jnp.int32), axis=1)
        kinetic = jnp.dot(weights[...], full.astype(BF16), preferred_element_type=F32)
        product[...] = kinetic + level * full[:ROWS, :]

    def spread(t, carry):
        e = first + t
        element(e)
        for b, start in enumerate(range(0, NPE, BATCH)):
            total = odd if b % 2 else even
            js = range(start, min(NPE, start + BATCH))
            at = [conn_ref[j, e] for j in js]
            sums = [total[pl.ds(i, 1), :] + product[pl.ds(j, 1), :] for i, j in zip(at, js)]
            for i, value in zip(at, sums):
                total[pl.ds(i, 1), :] = value
        return carry

    def spread_singly(t, carry):
        e = first + t
        element(e)

        def add(j, inner):
            i = conn_ref[j, e]
            even[pl.ds(i, 1), :] = even[pl.ds(i, 1), :] + product[pl.ds(j, 1), :]
            return inner

        lax.fori_loop(0, NPE, add, 0)
        return carry

    @pl.when(repeats == 0)
    def _():
        lax.fori_loop(0, HALF_CELLS, spread, 0)

    @pl.when(repeats != 0)
    def _():
        lax.fori_loop(0, HALF_CELLS, spread_singly, 0)

    lane = lax.broadcasted_iota(jnp.int32, (16, 128), 1)

    def pack(low, high, to):
        a = even[low, :] + odd[low, :]
        b = even[high, :] + odd[high, :]
        zero = jnp.where(lane < ORB, a, pltpu.roll(b, ORB, 1))
        one = jnp.where(lane < ORB, pltpu.roll(a, ORB, 1), b)
        own_ref[to, :] = jnp.where(core == 0, zero, one)
        leave_ref[to, :] = jnp.where(core == 0, one, zero).astype(BF16)

    def pack_nodes(r, carry):
        at = pl.multiple_of(r * 16, 16)
        pack(pl.ds(at, 16), pl.ds(LOW + at, 16), pl.ds(at, 16))
        return carry

    def pack_ghosts(r, carry):
        at = pl.multiple_of(r * 16, 16)
        pack(pl.ds(OWN + at, 16), pl.ds(OWN + HALF_GHOST + at, 16), pl.ds(LOW + at, 16))
        return carry

    lax.fori_loop(0, LOW // 16, pack_nodes, 0)
    lax.fori_loop(0, HALF_GHOST // 16, pack_ghosts, 0)


def elements(connectivity, potential, stiffness, table):
    return pl.pallas_call(
        element_kernel,
        out_shape=(jax.ShapeDtypeStruct((PACKED, 128), F32), jax.ShapeDtypeStruct((PACKED, 128), BF16)),
        in_specs=[SMEM, VMEM, VMEM, VMEM, VMEM],
        out_specs=(VMEM, VMEM),
        scratch_shapes=[
            pltpu.VMEM((LOCAL, 128), F32),
            pltpu.VMEM((LOCAL, 128), F32),
            pltpu.VMEM((DEEP, 128), F32),
            pltpu.VMEM((ROWS, 128), F32),
            pltpu.VMEM((ROWS, DEEP), BF16),
            pltpu.VMEM((ROWS, 128), F32),
        ],
        compiler_params=pltpu.CompilerParams(vmem_limit_bytes=56 * MIB),
    )(connectivity, connectivity, potential, stiffness, table)


def swap_kernel(own_ref, leave_ref, got_ref, in_ref, edge, other, leaving, sem, ss, sr):
    cell, core, peer, before, after = places()
    mine = pltpu.make_async_copy(own_ref.at[pl.ds(LOW, HALF_GHOST)], edge, sem)
    mine.start()
    greet([peer, before], 2)
    ghosts = remote(leave_ref.at[pl.ds(LOW, HALF_GHOST)], other, ss.at[0], sr.at[0], peer)
    ghosts.start()
    nodes = remote(leave_ref.at[pl.ds(0, LOW)], got_ref, ss.at[1], sr.at[1], peer)
    nodes.start()
    mine.wait()
    ghosts.wait_recv()
    leaving[...] = (edge[...] + other[...].astype(F32)).astype(BF16)
    shared = remote(leaving, in_ref, ss.at[2], sr.at[2], after)
    shared.start()
    nodes.wait_recv()
    shared.wait_recv()
    for copy in (ghosts, nodes, shared):
        copy.wait_send()


def swap(own, leave):
    return pl.pallas_call(
        swap_kernel,
        out_shape=(jax.ShapeDtypeStruct((LOW, 128), BF16), jax.ShapeDtypeStruct((HALF_GHOST, 128), BF16)),
        in_specs=[ANY, ANY],
        out_specs=(ANY, ANY),
        scratch_shapes=[
            pltpu.VMEM((HALF_GHOST, 128), F32),
            pltpu.VMEM((HALF_GHOST, 128), BF16),
            pltpu.VMEM((HALF_GHOST, 128), BF16),
            pltpu.SemaphoreType.DMA,
            pltpu.SemaphoreType.DMA((3,)),
            pltpu.SemaphoreType.DMA((3,)),
        ],
        compiler_params=pltpu.CompilerParams(collective_id=1, has_side_effects=True, vmem_limit_bytes=16 * MIB),
    )(own, leave)


def finish_kernel(bound_ref, own_ref, got_ref, in_ref, panels_ref, applied_ref, term_ref, nodes, ghosts):
    inner = lax.axis_index("cell") > 0

    def join(r, carry):
        at = pl.multiple_of(r * 128, 128)
        both = own_ref[pl.ds(at, 128), :] + got_ref[pl.ds(at, 128), :].astype(F32)
        nodes[pl.ds(at, 128), :] = both
        nodes[pl.ds(LOW + at, 128), :] = pltpu.roll(both, ORB, 1)
        return carry

    lax.fori_loop(0, LOW // 128, join, 0)
    edge = jnp.where(inner, in_ref[...].astype(F32), 0.0)
    ghosts[:HALF_GHOST, :] = edge
    ghosts[HALF_GHOST:, :] = pltpu.roll(edge, ORB, 1)

    def add(t, carry):
        at = t * 16
        to = [bound_ref[at + j] for j in range(16)]
        base = pl.multiple_of(at, 16)
        sums = [nodes[pl.ds(i, 1), :] + ghosts[pl.ds(base + j, 1), :] for j, i in enumerate(to)]
        for i, value in zip(to, sums):
            nodes[pl.ds(i, 1), :] = value
        return carry

    lax.fori_loop(0, GHOST // 16, add, 0)
    wide = 384
    term_ref[...] = jnp.zeros_like(term_ref)

    def turn(b, carry):
        at = pl.multiple_of(b * wide, 128)
        rounded = nodes[pl.ds(at, wide), :].astype(BF16)
        term_ref[...] += jnp.dot(panels_ref[:, pl.ds(at, wide)], rounded, preferred_element_type=F32)
        applied_ref[:, pl.ds(at, wide)] = nodes[pl.ds(at, wide), :].T[:ORB, :].astype(BF16)
        return carry

    lax.fori_loop(0, OWN // wide, turn, 0)


def finish(boundary, own, got, edge, panels):
    return pl.pallas_call(
        finish_kernel,
        out_shape=(jax.ShapeDtypeStruct((ORB, OWN), BF16), jax.ShapeDtypeStruct((PANELS, 128), F32)),
        in_specs=[SMEM, VMEM, VMEM, VMEM, VMEM],
        out_specs=(VMEM, VMEM),
        scratch_shapes=[pltpu.VMEM((2 * LOW, 128), F32), pltpu.VMEM((GHOST, 128), F32)],
        compiler_params=pltpu.CompilerParams(vmem_limit_bytes=56 * MIB),
    )(boundary, own, got, edge, panels)


def total_kernel(term_ref, out_ref, held, sem, ss, sr):
    cell = lax.axis_index("cell")
    barrier = pltpu.get_barrier_semaphore()

    def hail(d, carry):
        to = lax.rem(cell + d, N_CELL)
        pl.semaphore_signal(barrier, inc=1, device_id={"cell": to}, device_id_type=MESH)
        return carry

    lax.fori_loop(1, N_CELL, hail, 0)
    mine = pltpu.make_async_copy(term_ref.at[cell], held.at[0], sem)
    mine.start()
    pl.semaphore_wait(barrier, N_CELL - 1)

    def send(d, carry):
        to = lax.rem(cell + d, N_CELL)
        remote(term_ref.at[to], held.at[d], ss, sr, {"cell": to}).start()
        return carry

    lax.fori_loop(1, N_CELL, send, 0)
    rest = pl.ds(1, N_CELL - 1)
    every = remote(term_ref.at[rest], held.at[rest], ss, sr, {"cell": lax.rem(cell + 1, N_CELL)})
    mine.wait()
    every.wait()
    out_ref[...] = jnp.sum(held[...], axis=0)


def total(terms):
    return pl.pallas_call(
        total_kernel,
        out_shape=jax.ShapeDtypeStruct((2, 128), F32),
        in_specs=[VMEM],
        out_specs=VMEM,
        scratch_shapes=[
            pltpu.VMEM((N_CELL, 2, 128), F32),
            pltpu.SemaphoreType.DMA,
            pltpu.SemaphoreType.DMA,
            pltpu.SemaphoreType.DMA,
        ],
        compiler_params=pltpu.CompilerParams(collective_id=2, has_side_effects=True),
    )(terms)


def shards(orbitals, panels, stiffness, potential, connectivity, boundary):
    every_panel = lax.all_gather(panels, "orb", axis=0, tiled=True)
    table = collect(orbitals, boundary)
    own, leave = elements(connectivity, potential, stiffness, table)
    got, edge = swap(own, leave)
    applied, term = finish(boundary, own, got, edge, every_panel)
    block = total(term.reshape(N_CELL, PANELS // N_CELL, 128))
    return applied, block[:, :ORB]


def solution(mesh):
    return jax.shard_map(
        shards,
        mesh=mesh,
        in_specs=(
            P("orb", "cell"),
            P("orb", "cell"),
            P(),
            P(None, "cell"),
            P(None, "cell"),
            P("cell"),
        ),
        out_specs=(P("orb", "cell"), P("cell", "orb")),
        check_vma=False,
    )
```

time: 626 us -> 172 us (0.27)
  the two profiles are of different devices: /device:TPU:160 before, /device:TPU:32 now
where the time goes in v1:
time: 172 us
  Pallas kernels  143 us (83%)
  local copies, waits for them, and re-layouts  14.2 us (8%)
  between operations  14.1 us (8%)
    pallas_call x1, Pallas kernels, elements(): pl.pallas_call(element_kernel, out_shape=(jax.ShapeDtypeStruct((PACKED, 1...  60.6 us
    pallas_call x1, Pallas kernels, collect(): pl.pallas_call(collect_kernel, out_shape=jax.ShapeDtypeStruct((LOCAL, 2 *...  33.9 us
    pallas_call x1, Pallas kernels, swap(): pl.pallas_call(swap_kernel, out_shape=(jax.ShapeDtypeStruct((LOW, 128), B...  18.5 us
    pallas_call x1, Pallas kernels, finish(): pl.pallas_call(finish_kernel, out_shape=(jax.ShapeDtypeStruct((ORB, OWN),...  15.4 us
    unnamed x17, local copies, waits for them, and re-layouts  14.2 us
    pallas_call x1, Pallas kernels, total(): pl.pallas_call(total_kernel, out_shape=jax.ShapeDtypeStruct((2, 128), F32...  14.2 us
  transfers between devices with their start and end apart: 1, of which 0 were waited for; matrix products, arithmetic and copies ran while one was open for 2% of the time, Pallas kernels for 66%

profile of v1, /device:TPU:32, one launch (start us, length us, event | category | flops | bytes accessed | tf_op | source)
XLA Modules:
  0.0 171.6 jit_solution(5642031859079385263)
XLA Ops:
  7.2 0.0 all-gather.2.cloned.1.call-start
  7.2 0.7 all-gather.2.cloned.1.call-update
  7.9 1.7 copy.10.pot_ref
  9.6 1.7 copy.8.conn_ref.conn_vec
  11.3 0.0 copy-start.4
  11.3 1.3 copy-done.4
  12.6 0.0 copy-start.6
  12.6 0.7 copy-done.6
  13.3 33.9 %shard_map.77.table = f32[12096,128]{1,0:T(8,128)S(1)} custom-call(bf16[64,10368]{1,0:T(8,128)(2,1)S(1)} %copy-done.4, s32[1728]{0:T(1024)S(1)} %copy-done.6), custom_call_target="tpu_custom_call" | custom-call | tf_op jit(solution)/shard_map/pallas_call | solution.py:125
  47.2 0.0 copy-start
  47.2 2.6 %copy-done = f32[12096,128]{1,0:T(8,128)} copy-done((f32[12096,128]{1,0:T(8,128)}, f32[12096,128]{1,0:T(8,128)S(1)}, u32[]{:S(2)}) %copy-start) | copy-done | bytes 6193176
  49.8 60.6 %shard_map.78 = (f32[6112,128]{1,0:T(8,128)}, bf16[6112,128]{1,0:T(8,128)(2,1)}) custom-call(s32[343,48]{1,0:T(8,128)} %copy.8.conn_ref.conn_vec, s32[343,48]{1,0:T(8,128)} %copy.8.conn_ref.conn_vec, f32[343,48]{1,0:T(8,128)} %copy.10.pot_ref, bf16[343,343]{1,0:T(8,128)(2,1)} %stiff_ref.1, f32[12096,128]{1,0:T(8,128)} %copy-done), custom_call_target="tpu_custom_call" | custom-call | tf_op jit(solution)/shard_map/pallas_call | solution.py:231
  110.4 0.0 copy-start.1
  110.4 1.9 %copy-done.1 = f32[6112,128]{1,0:T(8,128)S(1)} copy-done((f32[6112,128]{1,0:T(8,128)S(1)}, f32[6112,128]{1,0:T(8,128)}, u32[]{:S(2)}) %copy-start.1) | copy-done | bytes 3129368
  112.2 0.0 copy-start.2
  112.2 1.4 copy-done.2
  113.6 18.5 %shard_map.79 = (bf16[5248,128]{1,0:T(8,128)(2,1)S(1)}, bf16[864,128]{1,0:T(8,128)(2,1)S(1)}) custom-call(f32[6112,128]{1,0:T(8,128)S(1)} %copy-done.1, bf16[6112,128]{1,0:T(8,128)(2,1)S(1)} %copy-done.2), custom_call_target="tpu_custom_call" | custom-call | tf_op jit(solution)/shard_map/pallas_call | solution.py:269
  132.2 0.0 copy-start.3
  132.2 1.1 copy-done.3
  133.3 0.0 copy-start.5
  133.3 0.7 copy-done.5
  134.0 15.4 %shard_map.80 = (bf16[64,10368]{1,0:T(8,128)(2,1)}, f32[128,128]{1,0:T(8,128)}) custom-call(s32[1728]{0:T(1024)} %bound_ref.3, f32[6112,128]{1,0:T(8,128)} %get-tuple-element.8.own_ref, bf16[5248,128]{1,0:T(8,128)(2,1)} %copy-done.3, bf16[864,128]{1,0:T(8,128)(2,1)} %copy-done.5, bf16[128,10368]{1,0:T(8,128)(2,1)} %all-gather.2.cloned.1.call-done.panels_ref), custom_call_target="tpu_custom_call" | custom-call | tf_op jit(solution)/shard_map/pallas_call | solution.py:325
  149.4 14.2 %shard_map.81 = f32[2,128]{1,0:T(2,128)} custom-call(f32[64,2,128]{2,1,0:T(2,128)} %bitcast.2), custom_call_target="tpu_custom_call" | custom-call | tf_op jit(solution)/shard_map/pallas_call | solution.py:363
  163.6 1.2 copy.12
  (1 shorter events, 0.0 us)
Async XLA Ops:
  7.2 126.8 %all-gather.2.cloned.1.call-start = ((), (), s32[]{:S(2)}) async-start(), calls=%async_computation | async-start | bytes 3317760 | tf_op jit(solution)/shard_map/all_gather | solution.py:379
  11.3 1.3 copy-start.4
  12.6 0.7 copy-start.6
  47.2 2.6 %copy-start = (f32[12096,128]{1,0:T(8,128)}, f32[12096,128]{1,0:T(8,128)S(1)}, u32[]{:S(2)}) copy-start(f32[12096,128]{1,0:T(8,128)S(1)} %shard_map.77.table) | copy-start | bytes 18579460
  110.4 1.9 %copy-start.1 = (f32[6112,128]{1,0:T(8,128)S(1)}, f32[6112,128]{1,0:T(8,128)}, u32[]{:S(2)}) copy-start(f32[6112,128]{1,0:T(8,128)} %get-tuple-element.8.own_ref) | copy-start | bytes 9388036
  112.2 1.4 copy-start.2
  132.2 1.1 copy-start.3
  133.3 0.7 copy-start.5
Sparse Core Ops, SparseCore 0:
  9.8 46.6 all-gather.1

commit v2 on v1

v2 whole, which is shorter than its diff:
```python
import jax
import jax.numpy as jnp
from jax import lax
from jax.experimental import pallas as pl
from jax.experimental.pallas import tpu as pltpu
from jax.sharding import PartitionSpec as P

ORB = 64
NPE = 343
ROWS = 344
DEEP = 384
CELLS = 48
HALF_CELLS = 24
OWN = 10368
GHOST = 1728
LOCAL = OWN + GHOST
PANELS = 128
N_CELL = 64
LOW = 5248
HALF_GHOST = 864
PACKED = LOW + HALF_GHOST
BATCH = 8
VMEM_LIMIT = 63 * 2**20
NODE_PACK = 656
GHOST_PACK = 432
TEAM = 4
ANY = pl.BlockSpec(memory_space=pltpu.HBM)
VMEM = pl.BlockSpec(memory_space=pltpu.VMEM)
SMEM = pl.BlockSpec(memory_space=pltpu.SMEM)
MESH = pl.DeviceIdType.MESH
F32 = jnp.float32
BF16 = jnp.bfloat16


def places():
    cell = lax.axis_index("cell")
    orb = lax.axis_index("orb")
    core = lax.rem(orb, 2)
    peer = {"orb": orb + 1 - 2 * core}
    before = {"cell": lax.rem(cell + N_CELL - 1, N_CELL)}
    after = {"cell": lax.rem(cell + 1, N_CELL)}
    return cell, core, peer, before, after


def greet(signalled, waits):
    barrier = pltpu.get_barrier_semaphore()
    for device in signalled:
        pl.semaphore_signal(barrier, inc=1, device_id=device, device_id_type=MESH)
    pl.semaphore_wait(barrier, waits)


def remote(src, dst, send, recv, device):
    return pltpu.make_async_remote_copy(
        src_ref=src, dst_ref=dst, send_sem=send, recv_sem=recv, device_id=device, device_id_type=MESH
    )


X_CHUNKS = 3
X_WIDE = OWN // X_CHUNKS
X_TURN = 1152
G_CHUNKS = 3
G_TURN = 96
G_ROWS = HALF_GHOST // G_CHUNKS


def collect_kernel(
    orb_ref, bound_ref, out_ref, x, table, rows, leaving, landed, local_sem, xs_sem, xr_sem, gs_sem, gr_sem, fs_sem, fr_sem, out_sem
):
    cell, core, peer, before, after = places()
    mine = pl.ds(pl.multiple_of(core * ORB, ORB), ORB)
    columns = [pl.ds(c * X_WIDE, X_WIDE) for c in range(X_CHUNKS)]
    own = [pltpu.make_async_copy(orb_ref.at[:, s], x.at[mine, s], local_sem.at[c]) for c, s in enumerate(columns)]
    for copy in own:
        copy.start()
    inner = cell < N_CELL - 1
    sends = cell > 0
    barrier = pltpu.get_barrier_semaphore()
    pl.semaphore_signal(barrier, inc=1, device_id=peer, device_id_type=MESH)

    @pl.when(inner)
    def _():
        pl.semaphore_signal(barrier, inc=1, device_id=after, device_id_type=MESH)

    pl.semaphore_wait(barrier, jnp.where(sends, 2, 1))
    given = [remote(orb_ref.at[:, s], x.at[mine, s], xs_sem.at[c], xr_sem.at[c], peer) for c, s in enumerate(columns)]
    for copy in given:
        copy.start()
    stored = []
    for c in range(X_CHUNKS):
        own[c].wait()
        given[c].wait_recv()

        def turn(b, carry, c=c):
            at = pl.multiple_of(c * X_WIDE + b * X_TURN, 128)
            table[pl.ds(at, X_TURN), :] = x[:, pl.ds(at, X_TURN)].T.astype(F32)
            return carry

        lax.fori_loop(0, X_WIDE // X_TURN, turn, 0)
        part = pl.ds(c * X_WIDE, X_WIDE)
        stored.append(pltpu.make_async_copy(table.at[part], out_ref.at[part], out_sem.at[c]))
        stored[-1].start()
    base = core * HALF_GHOST
    sent, passed = [], []
    for g in range(G_CHUNKS):

        def pick(t, carry, g=g):
            at = g * G_ROWS + t * G_TURN
            for j in range(G_TURN):
                rows[pl.ds(j, 1), :] = table[pl.ds(bound_ref[base + at + j], 1), :]
            leaving[pl.ds(pl.multiple_of(at, 16), G_TURN), :] = rows[...].astype(BF16)
            return carry

        src = pl.ds(g * G_ROWS, G_ROWS)
        dst = pl.ds(pl.multiple_of(base + g * G_ROWS, 16), G_ROWS)
        sent.append(remote(leaving.at[src], landed.at[dst], gs_sem.at[g], gr_sem.at[g], before))
        passed.append(remote(landed.at[dst], landed.at[dst], fs_sem.at[g], fr_sem.at[g], peer))

        @pl.when(sends)
        def _(pick=pick, g=g):
            lax.fori_loop(0, G_ROWS // G_TURN, pick, 0)
            sent[g].start()

    part = pl.ds(OWN, GHOST)
    stored.append(pltpu.make_async_copy(table.at[part], out_ref.at[part], out_sem.at[X_CHUNKS]))

    @pl.when(inner)
    def _():
        for g in range(G_CHUNKS):
            sent[g].wait_recv()
            passed[g].start()
        for copy in passed:
            copy.wait_recv()
        table[OWN:, :] = landed[...].astype(F32)
        for copy in passed:
            copy.wait_send()

    @pl.when(jnp.logical_not(inner))
    def _():
        table[OWN:, :] = jnp.zeros((GHOST, 2 * ORB), F32)

    stored[-1].start()
    for copy in given:
        copy.wait_send()

    @pl.when(sends)
    def _():
        for copy in sent:
            copy.wait_send()

    for copy in stored:
        copy.wait()


def collect(orbitals, boundary):
    dma = pltpu.SemaphoreType.DMA
    return pl.pallas_call(
        collect_kernel,
        out_shape=jax.ShapeDtypeStruct((LOCAL, 2 * ORB), F32),
        in_specs=[ANY, SMEM],
        out_specs=ANY,
        scratch_shapes=[
            pltpu.VMEM((2 * ORB, OWN), BF16),
            pltpu.VMEM((LOCAL, 2 * ORB), F32),
            pltpu.VMEM((G_TURN, 2 * ORB), F32),
            pltpu.VMEM((HALF_GHOST, 2 * ORB), BF16),
            pltpu.VMEM((GHOST, 2 * ORB), BF16),
            dma((X_CHUNKS,)),
            dma((X_CHUNKS,)),
            dma((X_CHUNKS,)),
            dma((G_CHUNKS,)),
            dma((G_CHUNKS,)),
            dma((G_CHUNKS,)),
            dma((G_CHUNKS,)),
            dma((X_CHUNKS + 1,)),
        ],
        compiler_params=pltpu.CompilerParams(collective_id=0, has_side_effects=True, vmem_limit_bytes=VMEM_LIMIT),
    )(orbitals, boundary)


def element_kernel(conn_ref, conn_vec, pot_ref, stiff_ref, table_ref, own_ref, leave_ref, table, leaving, even, odd, near, early, weights, scaled, scaled_t, sems):
    fetch = pltpu.make_async_copy(table_ref, table, sems.at[6])
    fetch.start()
    core = lax.rem(lax.axis_index("orb"), 2)
    first = core * HALF_CELLS
    even[...] = jnp.zeros_like(even)
    odd[...] = jnp.zeros_like(odd)
    near[:, NPE:, :] = jnp.zeros((TEAM, DEEP - NPE, 128), F32)
    weights[...] = jnp.zeros_like(weights)
    weights[:NPE, :NPE] = stiff_ref[...]
    scaled[...] = jnp.zeros_like(scaled)
    scaled[:CELLS, :NPE] = pot_ref[...]
    levels = scaled[...].T
    scaled_t[...] = levels

    alike = jnp.zeros((CELLS, 1), jnp.int32)
    for d in range(1, BATCH):
        same = conn_vec[:, : NPE - d] == conn_vec[:, d:NPE]
        alike = jnp.maximum(alike, jnp.max(same.astype(jnp.int32), axis=1, keepdims=True))
    repeats = jnp.max(alike)
    fetch.wait()

    def index(t, j):
        return conn_ref[(first + t) * NPE + j]

    def gather(t, js):
        for h in range(TEAM):
            for j in js:
                near[h, pl.ds(j, 1), :] = table[pl.ds(index(t + h, j), 1), :]

    def multiply(t):
        full = jnp.concatenate([near[h] for h in range(TEAM)], axis=1).astype(BF16)
        out = jnp.dot(weights[...], full, preferred_element_type=F32)
        for h in range(TEAM):
            level = jnp.take_along_axis(scaled_t[:ROWS, :], jnp.full((ROWS, 128), first + t + h, jnp.int32), axis=1)
            early[h] = out[:, h * 128 : h * 128 + 128] + level * near[h, :ROWS, :]

    def scatter(t, js):
        for h in range(TEAM):
            total = odd if h % 2 else even
            at = [index(t + h, j) for j in js]
            sums = [total[pl.ds(i, 1), :] + early[h, pl.ds(j, 1), :] for i, j in zip(at, js)]
            for i, value in zip(at, sums):
                total[pl.ds(i, 1), :] = value

    batches = [range(b, min(NPE, b + BATCH)) for b in range(0, NPE, BATCH)]

    def team(u, carry):
        t = TEAM * u
        for js in batches:
            gather(t, js)
            scatter(jnp.maximum(t - TEAM, 0), js)

        @pl.when(t >= 0)
        def _():
            multiply(t)

        return carry

    @pl.when(repeats == 0)
    def _():
        early[...] = jnp.zeros_like(early)
        lax.fori_loop(0, HALF_CELLS // TEAM, team, 0)
        for js in batches:
            scatter(HALF_CELLS - TEAM, js)

    @pl.when(repeats != 0)
    def _():
        def one(u, carry):
            def pick(j, inner):
                gather(TEAM * u, [j])
                return inner

            def add(j, inner):
                for h in range(TEAM):
                    i = index(TEAM * u + h, j)
                    even[pl.ds(i, 1), :] = even[pl.ds(i, 1), :] + early[h, pl.ds(j, 1), :]
                return inner

            lax.fori_loop(0, NPE, pick, 0)
            multiply(TEAM * u)
            lax.fori_loop(0, NPE, add, 0)
            return carry

        lax.fori_loop(0, HALF_CELLS // TEAM, one, 0)

    puts = []

    def pack(low, high, to, count):
        lane = lax.broadcasted_iota(jnp.int32, (count, 128), 1)
        straight = (lane < ORB) == (core == 0)
        low, high, to = (pl.ds(s, count) for s in (low, high, to))
        a = even[low, :] + odd[low, :]
        b = even[high, :] + odd[high, :]
        kept = jnp.where(lane < ORB, a, b)
        moved = pltpu.roll(jnp.where(lane < ORB, b, a), ORB, 1)
        table[to, :] = jnp.where(straight, kept, moved)
        leaving[to, :] = jnp.where(straight, moved, kept).astype(BF16)

    def put(start, count):
        part = pl.ds(start, count)
        puts.append(pltpu.make_async_copy(table.at[part], own_ref.at[part], sems.at[len(puts)]))
        puts[-1].start()
        puts.append(pltpu.make_async_copy(leaving.at[part], leave_ref.at[part], sems.at[len(puts)]))
        puts[-1].start()

    def pack_ghosts(r, carry):
        at = pl.multiple_of(r * GHOST_PACK, 16)
        pack(OWN + at, OWN + HALF_GHOST + at, LOW + at, GHOST_PACK)
        return carry

    def pack_nodes(r, carry):
        at = pl.multiple_of(r * NODE_PACK, 16)
        pack(at, LOW + at, at, NODE_PACK)
        return carry

    lax.fori_loop(0, HALF_GHOST // GHOST_PACK, pack_ghosts, 0)
    put(LOW, HALF_GHOST)
    turns = LOW // NODE_PACK
    lax.fori_loop(0, turns // 2, pack_nodes, 0)
    put(0, LOW // 2)
    lax.fori_loop(turns // 2, turns, pack_nodes, 0)
    put(LOW // 2, LOW // 2)
    for copy in puts:
        copy.wait()


def elements(connectivity, potential, stiffness, table):
    return pl.pallas_call(
        element_kernel,
        out_shape=(jax.ShapeDtypeStruct((PACKED, 128), F32), jax.ShapeDtypeStruct((PACKED, 128), BF16)),
        in_specs=[SMEM, VMEM, VMEM, VMEM, ANY],
        out_specs=(ANY, ANY),
        scratch_shapes=[
            pltpu.VMEM((LOCAL, 128), F32),
            pltpu.VMEM((PACKED, 128), BF16),
            pltpu.VMEM((LOCAL, 128), F32),
            pltpu.VMEM((LOCAL, 128), F32),
            pltpu.VMEM((TEAM, DEEP, 128), F32),
            pltpu.VMEM((TEAM, ROWS, 128), F32),
            pltpu.VMEM((ROWS, DEEP), BF16),
            pltpu.VMEM((128, DEEP), F32),
            pltpu.VMEM((DEEP, 128), F32),
            pltpu.SemaphoreType.DMA((7,)),
        ],
        compiler_params=pltpu.CompilerParams(vmem_limit_bytes=VMEM_LIMIT),
        cost_estimate=pl.CostEstimate(flops=2 * HALF_CELLS * NPE * NPE * 128, bytes_accessed=60 * 2**20, transcendentals=0),
    )(connectivity.T.reshape(-1), connectivity.T, potential.T, stiffness, table)


def swap_kernel(own_ref, leave_ref, panels_ref, far_ref, got_ref, in_ref, side_ref, edge, other, leaving, sem, ss, sr):
    cell, core, peer, before, after = places()
    mine = pltpu.make_async_copy(own_ref.at[pl.ds(LOW, HALF_GHOST)], edge, sem)
    mine.start()
    inner = cell > 0
    sends = cell < N_CELL - 1
    barrier = pltpu.get_barrier_semaphore()
    pl.semaphore_signal(barrier, inc=1, device_id=peer, device_id_type=MESH)

    @pl.when(inner)
    def _():
        pl.semaphore_signal(barrier, inc=1, device_id=before, device_id_type=MESH)

    pl.semaphore_wait(barrier, jnp.where(sends, 2, 1))
    ghosts = remote(leave_ref.at[pl.ds(LOW, HALF_GHOST)], other, ss.at[0], sr.at[0], peer)
    ghosts.start()
    nodes = remote(leave_ref.at[pl.ds(0, LOW)], got_ref, ss.at[1], sr.at[1], peer)
    nodes.start()
    rows = panels_ref.shape[0]
    near = remote(panels_ref, side_ref.at[pl.ds(0, rows)], ss.at[3], sr.at[3], peer)
    near.start()
    far = remote(far_ref, side_ref.at[pl.ds(rows, rows)], ss.at[4], sr.at[4], peer)
    far.start()
    mine.wait()
    ghosts.wait_recv()
    shared = remote(leaving, in_ref, ss.at[2], sr.at[2], after)

    @pl.when(sends)
    def _():
        leaving[...] = (edge[...] + other[...].astype(F32)).astype(BF16)
        shared.start()

    for copy in (nodes, near, far):
        copy.wait_recv()

    @pl.when(inner)
    def _():
        shared.wait_recv()

    for copy in (ghosts, nodes, near, far):
        copy.wait_send()

    @pl.when(sends)
    def _():
        shared.wait_send()


def swap(own, leave, panels, far):
    rows = panels.shape[0]
    return pl.pallas_call(
        swap_kernel,
        out_shape=(
            jax.ShapeDtypeStruct((LOW, 128), BF16),
            jax.ShapeDtypeStruct((HALF_GHOST, 128), BF16),
            jax.ShapeDtypeStruct((2 * rows, OWN), BF16),
        ),
        in_specs=[ANY, ANY, ANY, ANY],
        out_specs=(ANY, ANY, ANY),
        scratch_shapes=[
            pltpu.VMEM((HALF_GHOST, 128), F32),
            pltpu.VMEM((HALF_GHOST, 128), BF16),
            pltpu.VMEM((HALF_GHOST, 128), BF16),
            pltpu.SemaphoreType.DMA,
            pltpu.SemaphoreType.DMA((5,)),
            pltpu.SemaphoreType.DMA((5,)),
        ],
        compiler_params=pltpu.CompilerParams(collective_id=1, has_side_effects=True, vmem_limit_bytes=VMEM_LIMIT),
    )(own, leave, panels, far)


JOIN = 656
TURN = 1152
PICKS = 16
PICK_TURNS = 9


def finish_kernel(
    bound_ref, own_ref, got_ref, in_ref, mine_ref, far_ref, side_ref, applied_ref, term_ref, own, got, edge, panels, nodes, ghosts, turned, sems
):
    inner = lax.axis_index("cell") > 0
    gets = []
    for h in range(2):
        part = pl.ds(h * LOW // 2, LOW // 2)
        gets.append(pltpu.make_async_copy(own_ref.at[part], own.at[part], sems.at[2 * h]))
        gets.append(pltpu.make_async_copy(got_ref.at[part], got.at[part], sems.at[2 * h + 1]))
    gets.append(pltpu.make_async_copy(in_ref, edge, sems.at[4]))
    for copy in gets:
        copy.start()
    orb = lax.axis_index("orb")
    other, across = orb + 1 - 2 * lax.rem(orb, 2), lax.rem(orb + 2, 4)
    count = mine_ref.shape[0]
    sources = (mine_ref, far_ref, side_ref.at[pl.ds(0, count)], side_ref.at[pl.ds(count, count)])
    rows = (orb, across, other, lax.rem(other + 2, 4))
    parts = []
    for k, (source, row) in enumerate(zip(sources, rows)):
        to = panels.at[pl.ds(pl.multiple_of(row * count, count), count)]
        parts.append(pltpu.make_async_copy(source, to, sems.at[5 + k]))
        parts[-1].start()
    term_ref[...] = jnp.zeros_like(term_ref)

    def join(r, carry):
        at = pl.multiple_of(r * JOIN, 16)
        both = own[pl.ds(at, JOIN), :] + got[pl.ds(at, JOIN), :].astype(F32)
        nodes[pl.ds(at, JOIN), :] = both
        nodes[pl.ds(LOW + at, JOIN), :] = pltpu.roll(both, ORB, 1)
        return carry

    turns = LOW // JOIN
    gets[0].wait()
    gets[1].wait()
    lax.fori_loop(0, turns // 2, join, 0)
    gets[2].wait()
    gets[3].wait()
    lax.fori_loop(turns // 2, turns, join, 0)
    gets[4].wait()
    come = jnp.where(inner, edge[...].astype(F32), 0.0)
    ghosts[:HALF_GHOST, :] = come
    ghosts[HALF_GHOST:, :] = pltpu.roll(come, ORB, 1)
    count = GHOST // PICK_TURNS

    def add(t, carry):
        for p in range(0, count, PICKS):
            at = t * count + p
            to = [bound_ref[at + j] for j in range(PICKS)]
            base = pl.multiple_of(at, 16)
            sums = [nodes[pl.ds(i, 1), :] + ghosts[pl.ds(base + j, 1), :] for j, i in enumerate(to)]
            for i, value in zip(to, sums):
                nodes[pl.ds(i, 1), :] = value
        return carry

    lax.fori_loop(0, PICK_TURNS, add, 0)
    for copy in parts:
        copy.wait()

    def turn(b, carry):
        at = pl.multiple_of(b * TURN, 128)
        rounded = nodes[pl.ds(at, TURN), :].astype(BF16)
        term_ref[...] += jnp.dot(panels[:, pl.ds(at, TURN)], rounded, preferred_element_type=F32)
        turned[:, pl.ds(at, TURN)] = rounded.T[:ORB, :]
        return carry

    lax.fori_loop(0, OWN // TURN, turn, 0)
    whole = pltpu.make_async_copy(turned, applied_ref, sems.at[9])
    whole.start()
    whole.wait()


def finish(boundary, own, got, edge, panels, far, side):
    return pl.pallas_call(
        finish_kernel,
        out_shape=(jax.ShapeDtypeStruct((ORB, OWN), BF16), jax.ShapeDtypeStruct((PANELS, 128), F32)),
        in_specs=[SMEM, ANY, ANY, ANY, ANY, ANY, ANY],
        out_specs=(ANY, VMEM),
        scratch_shapes=[
            pltpu.VMEM((LOW, 128), F32),
            pltpu.VMEM((LOW, 128), BF16),
            pltpu.VMEM((HALF_GHOST, 128), BF16),
            pltpu.VMEM((PANELS, OWN), BF16),
            pltpu.VMEM((2 * LOW, 128), F32),
            pltpu.VMEM((GHOST, 128), F32),
            pltpu.VMEM((ORB, OWN), BF16),
            pltpu.SemaphoreType.DMA((10,)),
        ],
        compiler_params=pltpu.CompilerParams(vmem_limit_bytes=VMEM_LIMIT),
    )(boundary, own, got, edge, panels, far, side)


def total_kernel(term_ref, out_ref, far, mid, near, held_mid, held_near, ss, sr):
    cell = lax.axis_index("cell")
    z, y, x = cell // 16, lax.rem(cell // 4, 4), lax.rem(cell, 4)

    def at(axis, d):
        place = [z, y, x]
        place[axis] = lax.rem(place[axis] + d, 4)
        return place[axis], {"cell": place[0] * 16 + place[1] * 4 + place[2]}

    greet([at(axis, d)[1] for axis in range(3) for d in range(1, 4)], 9)

    def exchange(axis, source, landing):
        copies = []
        for d in range(1, 4):
            to, device = at(axis, d)
            copies.append(remote(source.at[to], landing.at[d - 1], ss.at[axis, d - 1], sr.at[axis, d - 1], device))
            copies[-1].start()
        for copy in copies:
            copy.wait_recv()
        return copies

    started = exchange(0, term_ref, far)
    some = term_ref[z] + (far[0] + far[1] + far[2])
    for q in range(4):
        held_mid[q] = some[8 * q : 8 * q + 8]
    started += exchange(1, held_mid, mid)
    few = held_mid[y] + (mid[0] + mid[1] + mid[2])
    for q in range(4):
        held_near[q] = few[2 * q : 2 * q + 2]
    started += exchange(2, held_near, near)
    out_ref[...] = (held_near[x] + (near[0] + near[1] + near[2]))[:, :ORB]
    for copy in started:
        copy.wait_send()


def total(terms):
    return pl.pallas_call(
        total_kernel,
        out_shape=jax.ShapeDtypeStruct((2, ORB), F32),
        in_specs=[VMEM],
        out_specs=VMEM,
        scratch_shapes=[
            pltpu.VMEM((3, 32, 128), F32),
            pltpu.VMEM((3, 8, 128), F32),
            pltpu.VMEM((3, 2, 128), F32),
            pltpu.VMEM((4, 8, 128), F32),
            pltpu.VMEM((4, 2, 128), F32),
            pltpu.SemaphoreType.DMA((3, 3)),
            pltpu.SemaphoreType.DMA((3, 3)),
        ],
        compiler_params=pltpu.CompilerParams(collective_id=2, has_side_effects=True, vmem_limit_bytes=VMEM_LIMIT),
    )(terms)


def shards(orbitals, panels, stiffness, potential, connectivity, boundary):
    table = collect(orbitals, boundary)
    panels, table = lax.optimization_barrier((panels, table))
    far = lax.ppermute(panels, "orb", [(0, 2), (2, 0), (1, 3), (3, 1)])
    own, leave = elements(connectivity, potential, stiffness, table)
    got, edge, side = swap(own, leave, panels, far)
    applied, term = finish(boundary, own, got, edge, panels, far, side)
    return applied, total(term.reshape(4, PANELS // 4, 128))


def solution(mesh):
    return jax.shard_map(
        shards,
        mesh=mesh,
        in_specs=(
            P("orb", "cell"),
            P("orb", "cell"),
            P(),
            P(None, "cell"),
            P(None, "cell"),
            P("cell"),
        ),
        out_specs=(P("orb", "cell"), P("cell", "orb")),
        check_vma=False,
    )
```

time: 172 us -> 98.6 us (0.57)
  the two profiles are of different devices: /device:TPU:32 before, /device:TPU:2 now
where the time goes in v2:
time: 98.6 us; the launch traced here: 98.3 us
  Pallas kernels  93.5 us (95%)
  local copies, waits for them, and re-layouts  2.04 us (2%)
  starting transfers between devices  2 us (2%)
    pallas_call x1, Pallas kernels, total(): pl.pallas_call(total_kernel, out_shape=jax.ShapeDtypeStruct((2, ORB), F32...  34.3 us
    pallas_call x1, Pallas kernels, elements(): pl.pallas_call(element_kernel, out_shape=(jax.ShapeDtypeStruct((PACKED, 1...  24.6 us
    pallas_call x1, Pallas kernels, collect(): pl.pallas_call(collect_kernel, out_shape=jax.ShapeDtypeStruct((LOCAL, 2 *...  14.8 us
    pallas_call x1, Pallas kernels, swap(): pl.pallas_call(swap_kernel, out_shape=(jax.ShapeDtypeStruct((LOW, 128), B...  10 us
    pallas_call x1, Pallas kernels, finish(): pl.pallas_call(finish_kernel, out_shape=(jax.ShapeDtypeStruct((ORB, OWN),...  9.84 us
    ppermute x1, starting transfers between devices, shards(): far = lax.ppermute(panels, 'orb', [(0, 2), (2, 0), (1, 3), (3, 1)])  2 us
  transfers between devices with their start and end apart: 1, of which 0 were waited for; matrix products, arithmetic and copies ran while one was open for 1% of the time, Pallas kernels for 25%

profile of v2, /device:TPU:2, one launch (start us, length us, event | category | flops | bytes accessed | tf_op | source)
XLA Modules:
  0.0 98.3 jit_solution(9637657595701283808)
XLA Ops:
  0.6 0.0 copy-start
  0.6 0.0 copy-start.1
  0.7 14.8 %shard_map.77.table_ref = f32[12096,128]{1,0:T(8,128)} custom-call(bf16[64,10368]{1,0:T(8,128)(2,1)} %orb_ref.1, s32[1728]{0:T(1024)} %bound_ref.3), custom_call_target="tpu_custom_call" | custom-call | tf_op jit(solution)/shard_map/pallas_call | solution.py:156
  15.4 0.0 copy-done
  15.4 2.0 %collective-permute-start = (bf16[32,10368]{1,0:T(8,128)(2,1)S(1)}, bf16[32,10368]{1,0:T(8,128)(2,1)}, u32[]{:S(2)}, u32[]{:S(2)}) collective-permute-start(bf16[32,10368]{1,0:T(8,128)(2,1)S(1)} %copy-done), channel_id=1, source_target_pairs={{0,2},{2,0},{1,3},{3,1},{4,6},{6,4},{5,7},{7,5},{8,10},{10,8},{9,1... | collective-permute-start | bytes 1990664 | tf_op jit(solution)/shard_map/ppermute | solution.py:554
  17.4 0.0 copy-done.1
  17.4 0.8 reshape.10.conn_ref
  18.2 24.6 %shard_map.78 = (f32[6112,128]{1,0:T(8,128)}, bf16[6112,128]{1,0:T(8,128)(2,1)}) custom-call(s32[16464]{0:T(1024)} %reshape.10.conn_ref, s32[48,343]{1,0:T(8,128)} %bitcast.3, f32[48,343]{1,0:T(8,128)} %bitcast.5, bf16[343,343]{1,0:T(8,128)(2,1)} %stiff_ref.1, f32[12096,128]{1,0:T(8,128)} %shard_map.77.table_ref), custom_call_target="tpu_custom_call" | custom-call | flops 722835456 | bytes 62914560 | tf_op jit(solution)/shard_map/pallas_call | solution.py:308
  42.9 0.0 collective-permute-done.far_ref
  42.9 10.0 %shard_map.79 = (bf16[5248,128]{1,0:T(8,128)(2,1)}, bf16[864,128]{1,0:T(8,128)(2,1)}, bf16[64,10368]{1,0:T(8,128)(2,1)}) custom-call(f32[6112,128]{1,0:T(8,128)} %get-tuple-element.12.own_ref, bf16[6112,128]{1,0:T(8,128)(2,1)} %get-tuple-element.13.leave_ref, bf16[32,10368]{1,0:T(8,128)(2,1)} %mine_ref, bf16[32,10368]{1,0:T(8,128)(2,1)} %collective-permute-done.far_ref), custom_call_target="tpu_custom_call" | custom-call | tf_op jit(solution)/shard_map/pallas_call | solution.py:379
  52.9 9.8 %shard_map.80 = (bf16[64,10368]{1,0:T(8,128)(2,1)}, f32[128,128]{1,0:T(8,128)}) custom-call(s32[1728]{0:T(1024)} %bound_ref.3, f32[6112,128]{1,0:T(8,128)} %get-tuple-element.12.own_ref, bf16[5248,128]{1,0:T(8,128)(2,1)} %get-tuple-element.15.got_ref, bf16[864,128]{1,0:T(8,128)(2,1)} %get-tuple-element.16.in_ref, bf16[32,10368]{1,0:T(8,128)(2,1)} %mine_ref, ...), custom_call_target="tpu_custom_call" | custom-call | tf_op jit(solution)/shard_map/pallas_call | solution.py:478
  62.8 34.3 %shard_map.81 = f32[2,64]{1,0:T(2,128)} custom-call(f32[4,32,128]{2,1,0:T(8,128)} %bitcast.6), custom_call_target="tpu_custom_call" | custom-call | tf_op jit(solution)/shard_map/pallas_call | solution.py:533
  97.0 1.2 %copy.9 = f32[2,64]{1,0:T(2,128)} copy(f32[2,64]{1,0:T(2,128)} %shard_map.81) | data formatting | bytes 1024
Async XLA Ops:
  0.6 14.8 %copy-start = (bf16[32,10368]{1,0:T(8,128)(2,1)S(1)}, bf16[32,10368]{1,0:T(8,128)(2,1)}, u32[]{:S(2)}) copy-start(bf16[32,10368]{1,0:T(8,128)(2,1)} %mine_ref) | copy-start | bytes 1990660
  0.6 16.8 %copy-start.1 = (s32[343,48]{0,1:T(8,128)S(1)}, s32[343,48]{0,1:T(8,128)}, u32[]{:S(2)}) copy-start(s32[343,48]{0,1:T(8,128)} %param.10) | copy-start | bytes 197572
  15.4 27.4 %collective-permute-start = (bf16[32,10368]{1,0:T(8,128)(2,1)S(1)}, bf16[32,10368]{1,0:T(8,128)(2,1)}, u32[]{:S(2)}, u32[]{:S(2)}) collective-permute-start(bf16[32,10368]{1,0:T(8,128)(2,1)S(1)} %copy-done), channel_id=1, source_target_pairs={{0,2},{2,0},{1,3},{3,1},{4,6},{6,4},{5,7},{7,5},{8,10},{10,8},{9,1... | collective-permute-start | bytes 1990664 | tf_op jit(solution)/shard_map/ppermute | solution.py:554

commit v3 on v2

--- a/solution.py
+++ b/solution.py
@@ -59,21 +59,21 @@
 X_WIDE = OWN // X_CHUNKS
 X_TURN = 1152
 G_CHUNKS = 3
-G_TURN = 96
 G_ROWS = HALF_GHOST // G_CHUNKS
+G_TURN = 48
 
 
 def collect_kernel(
-    orb_ref, bound_ref, out_ref, x, table, rows, leaving, landed, local_sem, xs_sem, xr_sem, gs_sem, gr_sem, fs_sem, fr_sem, out_sem
+    orb_ref, bound_ref, out_ref, x, table, alone, low, high, leaving, landed, local_sem, xs_sem, xr_sem, gs_sem, gr_sem, fs_sem, fr_sem, out_sem
 ):
     cell, core, peer, before, after = places()
+    inner = cell < N_CELL - 1
+    sends = cell > 0
     mine = pl.ds(pl.multiple_of(core * ORB, ORB), ORB)
     columns = [pl.ds(c * X_WIDE, X_WIDE) for c in range(X_CHUNKS)]
     own = [pltpu.make_async_copy(orb_ref.at[:, s], x.at[mine, s], local_sem.at[c]) for c, s in enumerate(columns)]
     for copy in own:
         copy.start()
-    inner = cell < N_CELL - 1
-    sends = cell > 0
     barrier = pltpu.get_barrier_semaphore()
     pl.semaphore_signal(barrier, inc=1, device_id=peer, device_id_type=MESH)
 
@@ -81,13 +81,48 @@
     def _():
         pl.semaphore_signal(barrier, inc=1, device_id=after, device_id_type=MESH)
 
-    pl.semaphore_wait(barrier, jnp.where(sends, 2, 1))
-    given = [remote(orb_ref.at[:, s], x.at[mine, s], xs_sem.at[c], xr_sem.at[c], peer) for c, s in enumerate(columns)]
-    for copy in given:
-        copy.start()
+    for c in range(X_CHUNKS):
+        own[c].wait()
+
+        def turn_own(b, carry, c=c):
+            at = pl.multiple_of(c * X_WIDE + b * X_TURN, 128)
+            alone[pl.ds(at, X_TURN), :ORB] = x[mine, pl.ds(at, X_TURN)].T.astype(F32)
+            return carry
+
+        lax.fori_loop(0, X_WIDE // X_TURN, turn_own, 0)
+
+    lane = lax.broadcasted_iota(jnp.int32, (G_TURN, 2 * ORB), 1)
+    sent, passed, given = [], [], []
+    for g in range(G_CHUNKS):
+
+        def pick(t, carry, g=g):
+            at = g * G_ROWS + t * G_TURN
+            for j in range(G_TURN):
+                low[pl.ds(j, 1), :] = alone[pl.ds(bound_ref[at + j], 1), :]
+                high[pl.ds(j, 1), :] = alone[pl.ds(bound_ref[HALF_GHOST + at + j], 1), :]
+            both = jnp.where(lane < ORB, low[...], pltpu.roll(high[...], ORB, 1))
+            leaving[pl.ds(pl.multiple_of(at, 16), G_TURN), :] = both.astype(BF16)
+            return carry
+
+        part = pl.ds(g * G_ROWS, G_ROWS)
+        sent.append(remote(leaving.at[part], landed.at[core, part], gs_sem.at[g], gr_sem.at[g], before))
+        passed.append(remote(landed.at[core, part], landed.at[core, part], fs_sem.at[g], fr_sem.at[g], peer))
+
+        @pl.when(sends)
+        def _(pick=pick):
+            lax.fori_loop(0, G_ROWS // G_TURN, pick, 0)
+
+        if g == 0:
+            pl.semaphore_wait(barrier, jnp.where(sends, 2, 1))
+
+        @pl.when(sends)
+        def _(g=g):
+            sent[g].start()
+
+        given.append(remote(orb_ref.at[:, columns[g]], x.at[mine, columns[g]], xs_sem.at[g], xr_sem.at[g], peer))
+        given[g].start()
     stored = []
     for c in range(X_CHUNKS):
-        own[c].wait()
         given[c].wait_recv()
 
         def turn(b, carry, c=c):
@@ -99,27 +134,6 @@
         part = pl.ds(c * X_WIDE, X_WIDE)
         stored.append(pltpu.make_async_copy(table.at[part], out_ref.at[part], out_sem.at[c]))
         stored[-1].start()
-    base = core * HALF_GHOST
-    sent, passed = [], []
-    for g in range(G_CHUNKS):
-
-        def pick(t, carry, g=g):
-            at = g * G_ROWS + t * G_TURN
-            for j in range(G_TURN):
-                rows[pl.ds(j, 1), :] = table[pl.ds(bound_ref[base + at + j], 1), :]
-            leaving[pl.ds(pl.multiple_of(at, 16), G_TURN), :] = rows[...].astype(BF16)
-            return carry
-
-        src = pl.ds(g * G_ROWS, G_ROWS)
-        dst = pl.ds(pl.multiple_of(base + g * G_ROWS, 16), G_ROWS)
-        sent.append(remote(leaving.at[src], landed.at[dst], gs_sem.at[g], gr_sem.at[g], before))
-        passed.append(remote(landed.at[dst], landed.at[dst], fs_sem.at[g], fr_sem.at[g], peer))
-
-        @pl.when(sends)
-        def _(pick=pick, g=g):
-            lax.fori_loop(0, G_ROWS // G_TURN, pick, 0)
-            sent[g].start()
-
     part = pl.ds(OWN, GHOST)
     stored.append(pltpu.make_async_copy(table.at[part], out_ref.at[part], out_sem.at[X_CHUNKS]))
 
@@ -128,9 +142,13 @@
         for g in range(G_CHUNKS):
             sent[g].wait_recv()
             passed[g].start()
-        for copy in passed:
-            copy.wait_recv()
-        table[OWN:, :] = landed[...].astype(F32)
+        for g in range(G_CHUNKS):
+            passed[g].wait_recv()
+            rows = pl.ds(g * G_ROWS, G_ROWS)
+            zero, one = landed[0, rows, :].astype(F32), landed[1, rows, :].astype(F32)
+            first = lax.broadcasted_iota(jnp.int32, (G_ROWS, 2 * ORB), 1) < ORB
+            table[pl.ds(OWN + g * G_ROWS, G_ROWS), :] = jnp.where(first, zero, pltpu.roll(one, ORB, 1))
+            table[pl.ds(OWN + HALF_GHOST + g * G_ROWS, G_ROWS), :] = jnp.where(first, pltpu.roll(zero, ORB, 1), one)
         for copy in passed:
             copy.wait_send()
 
@@ -161,9 +179,11 @@
         scratch_shapes=[
             pltpu.VMEM((2 * ORB, OWN), BF16),
             pltpu.VMEM((LOCAL, 2 * ORB), F32),
+            pltpu.VMEM((OWN, 2 * ORB), F32),
+            pltpu.VMEM((G_TURN, 2 * ORB), F32),
             pltpu.VMEM((G_TURN, 2 * ORB), F32),
             pltpu.VMEM((HALF_GHOST, 2 * ORB), BF16),
-            pltpu.VMEM((GHOST, 2 * ORB), BF16),
+            pltpu.VMEM((2, HALF_GHOST, 2 * ORB), BF16),
             dma((X_CHUNKS,)),
             dma((X_CHUNKS,)),
             dma((X_CHUNKS,)),
@@ -177,9 +197,11 @@
     )(orbitals, boundary)
 
 
-def element_kernel(conn_ref, conn_vec, pot_ref, stiff_ref, table_ref, own_ref, leave_ref, table, leaving, even, odd, near, early, weights, scaled, scaled_t, sems):
+def element_kernel(conn_hbm, conn_vec, pot_ref, stiff_ref, table_ref, own_ref, leave_ref, table, leaving, even, odd, near, early, weights, scaled, scaled_t, sems, conn_ref, list_sem):
     fetch = pltpu.make_async_copy(table_ref, table, sems.at[6])
     fetch.start()
+    list_copy = pltpu.make_async_copy(conn_hbm, conn_ref, list_sem)
+    list_copy.start()
     core = lax.rem(lax.axis_index("orb"), 2)
     first = core * HALF_CELLS
     even[...] = jnp.zeros_like(even)
@@ -198,12 +220,13 @@
         alike = jnp.maximum(alike, jnp.max(same.astype(jnp.int32), axis=1, keepdims=True))
     repeats = jnp.max(alike)
     fetch.wait()
+    list_copy.wait()
 
     def index(t, j):
         return conn_ref[(first + t) * NPE + j]
 
-    def gather(t, js):
-        for h in range(TEAM):
+    def gather(t, js, team=range(TEAM)):
+        for h in team:
             for j in js:
                 near[h, pl.ds(j, 1), :] = table[pl.ds(index(t + h, j), 1), :]
 
@@ -214,8 +237,8 @@
             level = jnp.take_along_axis(scaled_t[:ROWS, :], jnp.full((ROWS, 128), first + t + h, jnp.int32), axis=1)
             early[h] = out[:, h * 128 : h * 128 + 128] + level * near[h, :ROWS, :]
 
-    def scatter(t, js):
-        for h in range(TEAM):
+    def scatter(t, js, team=range(TEAM)):
+        for h in team:
             total = odd if h % 2 else even
             at = [index(t + h, j) for j in js]
             sums = [total[pl.ds(i, 1), :] + early[h, pl.ds(j, 1), :] for i, j in zip(at, js)]
@@ -227,8 +250,9 @@
     def team(u, carry):
         t = TEAM * u
         for js in batches:
-            gather(t, js)
-            scatter(jnp.maximum(t - TEAM, 0), js)
+            for h in range(TEAM):
+                gather(t, js, [h])
+                scatter(jnp.maximum(t - TEAM, 0), js, [h])
 
         @pl.when(t >= 0)
         def _():
@@ -308,7 +332,7 @@
     return pl.pallas_call(
         element_kernel,
         out_shape=(jax.ShapeDtypeStruct((PACKED, 128), F32), jax.ShapeDtypeStruct((PACKED, 128), BF16)),
-        in_specs=[SMEM, VMEM, VMEM, VMEM, ANY],
+        in_specs=[ANY, VMEM, VMEM, VMEM, ANY],
         out_specs=(ANY, ANY),
         scratch_shapes=[
             pltpu.VMEM((LOCAL, 128), F32),
@@ -321,13 +345,15 @@
             pltpu.VMEM((128, DEEP), F32),
             pltpu.VMEM((DEEP, 128), F32),
             pltpu.SemaphoreType.DMA((7,)),
+            pltpu.SMEM((CELLS * NPE,), jnp.int32),
+            pltpu.SemaphoreType.DMA,
         ],
         compiler_params=pltpu.CompilerParams(vmem_limit_bytes=VMEM_LIMIT),
         cost_estimate=pl.CostEstimate(flops=2 * HALF_CELLS * NPE * NPE * 128, bytes_accessed=60 * 2**20, transcendentals=0),
     )(connectivity.T.reshape(-1), connectivity.T, potential.T, stiffness, table)
 
 
-def swap_kernel(own_ref, leave_ref, panels_ref, far_ref, got_ref, in_ref, side_ref, edge, other, leaving, sem, ss, sr):
+def swap_kernel(own_ref, leave_ref, panels_ref, far_ref, got_ref, in_ref, side_ref, edge, other, leaving, sem, ss, sr, gs, gr, es, er):
     cell, core, peer, before, after = places()
     mine = pltpu.make_async_copy(own_ref.at[pl.ds(LOW, HALF_GHOST)], edge, sem)
     mine.start()
@@ -341,37 +367,44 @@
         pl.semaphore_signal(barrier, inc=1, device_id=before, device_id_type=MESH)
 
     pl.semaphore_wait(barrier, jnp.where(sends, 2, 1))
-    ghosts = remote(leave_ref.at[pl.ds(LOW, HALF_GHOST)], other, ss.at[0], sr.at[0], peer)
-    ghosts.start()
-    nodes = remote(leave_ref.at[pl.ds(0, LOW)], got_ref, ss.at[1], sr.at[1], peer)
+    ghosts, shared = [], []
+    for g in range(G_CHUNKS):
+        part = pl.ds(g * G_ROWS, G_ROWS)
+        ghosts.append(remote(leave_ref.at[pl.ds(LOW + g * G_ROWS, G_ROWS)], other.at[part], gs.at[g], gr.at[g], peer))
+        ghosts[-1].start()
+        shared.append(remote(leaving.at[part], in_ref.at[part], es.at[g], er.at[g], after))
+    nodes = remote(leave_ref.at[pl.ds(0, LOW)], got_ref, ss.at[0], sr.at[0], peer)
     nodes.start()
     rows = panels_ref.shape[0]
-    near = remote(panels_ref, side_ref.at[pl.ds(0, rows)], ss.at[3], sr.at[3], peer)
+    near = remote(panels_ref, side_ref.at[pl.ds(0, rows)], ss.at[1], sr.at[1], peer)
     near.start()
-    far = remote(far_ref, side_ref.at[pl.ds(rows, rows)], ss.at[4], sr.at[4], peer)
+    far = remote(far_ref, side_ref.at[pl.ds(rows, rows)], ss.at[2], sr.at[2], peer)
     far.start()
     mine.wait()
-    ghosts.wait_recv()
-    shared = remote(leaving, in_ref, ss.at[2], sr.at[2], after)
-
-    @pl.when(sends)
-    def _():
-        leaving[...] = (edge[...] + other[...].astype(F32)).astype(BF16)
-        shared.start()
+    for g in range(G_CHUNKS):
+        ghosts[g].wait_recv()
+        part = pl.ds(g * G_ROWS, G_ROWS)
+
+        @pl.when(sends)
+        def _(g=g, part=part):
+            leaving[part, :] = (edge[part, :] + other[part, :].astype(F32)).astype(BF16)
+            shared[g].start()
 
     for copy in (nodes, near, far):
         copy.wait_recv()
 
     @pl.when(inner)
     def _():
-        shared.wait_recv()
-
-    for copy in (ghosts, nodes, near, far):
+        for copy in shared:
+            copy.wait_recv()
+
+    for copy in [*ghosts, nodes, near, far]:
         copy.wait_send()
 
     @pl.when(sends)
     def _():
-        shared.wait_send()
+        for copy in shared:
+            copy.wait_send()
 
 
 def swap(own, leave, panels, far):
@@ -390,8 +423,12 @@
             pltpu.VMEM((HALF_GHOST, 128), BF16),
             pltpu.VMEM((HALF_GHOST, 128), BF16),
             pltpu.SemaphoreType.DMA,
-            pltpu.SemaphoreType.DMA((5,)),
-            pltpu.SemaphoreType.DMA((5,)),
+            pltpu.SemaphoreType.DMA((3,)),
+            pltpu.SemaphoreType.DMA((3,)),
+            pltpu.SemaphoreType.DMA((G_CHUNKS,)),
+            pltpu.SemaphoreType.DMA((G_CHUNKS,)),
+            pltpu.SemaphoreType.DMA((G_CHUNKS,)),
+            pltpu.SemaphoreType.DMA((G_CHUNKS,)),
         ],
         compiler_params=pltpu.CompilerParams(collective_id=1, has_side_effects=True, vmem_limit_bytes=VMEM_LIMIT),
     )(own, leave, panels, far)
@@ -461,17 +498,16 @@
     for copy in parts:
         copy.wait()
 
-    def turn(b, carry):
-        at = pl.multiple_of(b * TURN, 128)
-        rounded = nodes[pl.ds(at, TURN), :].astype(BF16)
-        term_ref[...] += jnp.dot(panels[:, pl.ds(at, TURN)], rounded, preferred_element_type=F32)
-        turned[:, pl.ds(at, TURN)] = rounded.T[:ORB, :]
-        return carry
-
-    lax.fori_loop(0, OWN // TURN, turn, 0)
-    whole = pltpu.make_async_copy(turned, applied_ref, sems.at[9])
-    whole.start()
-    whole.wait()
+    puts = []
+    for b in range(OWN // TURN):
+        part = pl.ds(b * TURN, TURN)
+        rounded = nodes[part, :].astype(BF16)
+        term_ref[...] += jnp.dot(panels[:, part], rounded, preferred_element_type=F32)
+        turned[:, part] = rounded.T[:ORB, :]
+        puts.append(pltpu.make_async_copy(turned.at[:, part], applied_ref.at[:, part], sems.at[9 + b]))
+        puts[-1].start()
+    for copy in puts:
+        copy.wait()
 
 
 def finish(boundary, own, got, edge, panels, far, side):
@@ -488,7 +524,7 @@
             pltpu.VMEM((2 * LOW, 128), F32),
             pltpu.VMEM((GHOST, 128), F32),
             pltpu.VMEM((ORB, OWN), BF16),
-            pltpu.SemaphoreType.DMA((10,)),
+            pltpu.SemaphoreType.DMA((9 + OWN // TURN,)),
         ],
         compiler_params=pltpu.CompilerParams(vmem_limit_bytes=VMEM_LIMIT),
     )(boundary, own, got, edge, panels, far, side)

time: 98.6 us -> 92.3 us (0.936)
  Pallas kernels: 93.5 us -> 87.3 us
    pallas_call x1, Pallas kernels: 34.3 us -> 32.1 us  [total(): pl.pallas_call(total_kernel, out_shape=jax.ShapeDtypeStruct((2, ORB), F32...]
    pallas_call x1, Pallas kernels: 14.8 us -> 13.1 us  [collect(): pl.pallas_call(collect_kernel, out_shape=jax.ShapeDtypeStruct((LOCAL, 2 *...]
    pallas_call x1, Pallas kernels: 9.84 us -> 8.29 us  [finish(): pl.pallas_call(finish_kernel, out_shape=(jax.ShapeDtypeStruct((ORB, OWN),...]
  transfers between devices with their start and end apart: 1 -> 1, of which waited for: 0 -> 0; matrix products, arithmetic and copies ran while one was open for 1% -> 1% of each run, Pallas kernels for 25% -> 26%
where the time goes in v3:
time: 92.3 us; the launch traced here: 92.1 us
  Pallas kernels  87.3 us (95%)
  local copies, waits for them, and re-layouts  2.04 us (2%)
  starting transfers between devices  2 us (2%)
    pallas_call x1, Pallas kernels, total(): pl.pallas_call(total_kernel, out_shape=jax.ShapeDtypeStruct((2, ORB), F32...  32.1 us
    pallas_call x1, Pallas kernels, elements(): pl.pallas_call(element_kernel, out_shape=(jax.ShapeDtypeStruct((PACKED, 1...  24.2 us
    pallas_call x1, Pallas kernels, collect(): pl.pallas_call(collect_kernel, out_shape=jax.ShapeDtypeStruct((LOCAL, 2 *...  13.1 us
    pallas_call x1, Pallas kernels, swap(): pl.pallas_call(swap_kernel, out_shape=(jax.ShapeDtypeStruct((LOW, 128), B...  9.65 us
    pallas_call x1, Pallas kernels, finish(): pl.pallas_call(finish_kernel, out_shape=(jax.ShapeDtypeStruct((ORB, OWN),...  8.29 us
    ppermute x1, starting transfers between devices, shards(): far = lax.ppermute(panels, 'orb', [(0, 2), (2, 0), (1, 3), (3, 1)])  2 us
  transfers between devices with their start and end apart: 1, of which 0 were waited for; matrix products, arithmetic and copies ran while one was open for 1% of the time, Pallas kernels for 26%

profile of v3, /device:TPU:2, one launch (start us, length us, event | category | flops | bytes accessed | tf_op | source)
XLA Modules:
  0.0 92.1 jit_solution(3341432603806610418)
XLA Ops:
  0.6 0.0 copy-start
  0.6 0.0 copy-start.1
  0.7 13.1 %shard_map.77.table_ref = f32[12096,128]{1,0:T(8,128)} custom-call(bf16[64,10368]{1,0:T(8,128)(2,1)} %orb_ref.1, s32[1728]{0:T(1024)} %bound_ref.3), custom_call_target="tpu_custom_call" | custom-call | tf_op jit(solution)/shard_map/pallas_call | solution.py:174
  13.8 0.0 copy-done
  13.8 2.0 %collective-permute-start = (bf16[32,10368]{1,0:T(8,128)(2,1)S(1)}, bf16[32,10368]{1,0:T(8,128)(2,1)}, u32[]{:S(2)}, u32[]{:S(2)}) collective-permute-start(bf16[32,10368]{1,0:T(8,128)(2,1)S(1)} %copy-done), channel_id=1, source_target_pairs={{0,2},{2,0},{1,3},{3,1},{4,6},{6,4},{5,7},{7,5},{8,10},{10,8},{9,1... | collective-permute-start | bytes 1990664 | tf_op jit(solution)/shard_map/ppermute | solution.py:590
  15.8 0.0 copy-done.1
  15.8 0.8 reshape.10.conn_hbm
  16.6 24.2 %shard_map.78 = (f32[6112,128]{1,0:T(8,128)}, bf16[6112,128]{1,0:T(8,128)(2,1)}) custom-call(s32[16464]{0:T(1024)} %reshape.10.conn_hbm, s32[48,343]{1,0:T(8,128)} %bitcast.3, f32[48,343]{1,0:T(8,128)} %bitcast.5, bf16[343,343]{1,0:T(8,128)(2,1)} %stiff_ref.1, f32[12096,128]{1,0:T(8,128)} %shard_map.77.table_ref), custom_call_target="tpu_custom_call" | custom-call | flops 722835456 | bytes 62914560 | tf_op jit(solution)/shard_map/pallas_call | solution.py:332
  40.8 0.0 collective-permute-done.far_ref
  40.8 9.6 %shard_map.79 = (bf16[5248,128]{1,0:T(8,128)(2,1)}, bf16[864,128]{1,0:T(8,128)(2,1)}, bf16[64,10368]{1,0:T(8,128)(2,1)}) custom-call(f32[6112,128]{1,0:T(8,128)} %get-tuple-element.12.own_ref, bf16[6112,128]{1,0:T(8,128)(2,1)} %get-tuple-element.13.leave_ref, bf16[32,10368]{1,0:T(8,128)(2,1)} %mine_ref, bf16[32,10368]{1,0:T(8,128)(2,1)} %collective-permute-done.far_ref), custom_call_target="tpu_custom_call" | custom-call | tf_op jit(solution)/shard_map/pallas_call | solution.py:412
  50.4 8.3 %shard_map.80 = (bf16[64,10368]{1,0:T(8,128)(2,1)}, f32[128,128]{1,0:T(8,128)}) custom-call(s32[1728]{0:T(1024)} %bound_ref.3, f32[6112,128]{1,0:T(8,128)} %get-tuple-element.12.own_ref, bf16[5248,128]{1,0:T(8,128)(2,1)} %get-tuple-element.15.got_ref, bf16[864,128]{1,0:T(8,128)(2,1)} %get-tuple-element.16.in_ref, bf16[32,10368]{1,0:T(8,128)(2,1)} %mine_ref, ...), custom_call_target="tpu_custom_call" | custom-call | tf_op jit(solution)/shard_map/pallas_call | solution.py:514
  58.7 32.1 %shard_map.81 = f32[2,64]{1,0:T(2,128)} custom-call(f32[4,32,128]{2,1,0:T(8,128)} %bitcast.6), custom_call_target="tpu_custom_call" | custom-call | tf_op jit(solution)/shard_map/pallas_call | solution.py:569
  90.8 1.2 %copy.9 = f32[2,64]{1,0:T(2,128)} copy(f32[2,64]{1,0:T(2,128)} %shard_map.81) | data formatting | bytes 1024
Async XLA Ops:
  0.6 13.1 %copy-start = (bf16[32,10368]{1,0:T(8,128)(2,1)S(1)}, bf16[32,10368]{1,0:T(8,128)(2,1)}, u32[]{:S(2)}) copy-start(bf16[32,10368]{1,0:T(8,128)(2,1)} %mine_ref) | copy-start | bytes 1990660
  0.6 15.1 %copy-start.1 = (s32[343,48]{0,1:T(8,128)S(1)}, s32[343,48]{0,1:T(8,128)}, u32[]{:S(2)}) copy-start(s32[343,48]{0,1:T(8,128)} %param.10) | copy-start | bytes 197572
  13.8 27.0 %collective-permute-start = (bf16[32,10368]{1,0:T(8,128)(2,1)S(1)}, bf16[32,10368]{1,0:T(8,128)(2,1)}, u32[]{:S(2)}, u32[]{:S(2)}) collective-permute-start(bf16[32,10368]{1,0:T(8,128)(2,1)S(1)} %copy-done), channel_id=1, source_target_pairs={{0,2},{2,0},{1,3},{3,1},{4,6},{6,4},{5,7},{7,5},{8,10},{10,8},{9,1... | collective-permute-start | bytes 1990664 | tf_op jit(solution)/shard_map/ppermute | solution.py:590

commit v4 on v3

--- a/solution.py
+++ b/solution.py
@@ -530,38 +530,34 @@
     )(boundary, own, got, edge, panels, far, side)
 
 
-def total_kernel(term_ref, out_ref, far, mid, near, held_mid, held_near, ss, sr):
+PLANE = 16
+
+
+def total_kernel(term_ref, out_ref, far, near, held, far_s, far_r, near_s, near_r):
     cell = lax.axis_index("cell")
-    z, y, x = cell // 16, lax.rem(cell // 4, 4), lax.rem(cell, 4)
-
-    def at(axis, d):
-        place = [z, y, x]
-        place[axis] = lax.rem(place[axis] + d, 4)
-        return place[axis], {"cell": place[0] * 16 + place[1] * 4 + place[2]}
-
-    greet([at(axis, d)[1] for axis in range(3) for d in range(1, 4)], 9)
-
-    def exchange(axis, source, landing):
-        copies = []
-        for d in range(1, 4):
-            to, device = at(axis, d)
-            copies.append(remote(source.at[to], landing.at[d - 1], ss.at[axis, d - 1], sr.at[axis, d - 1], device))
-            copies[-1].start()
-        for copy in copies:
-            copy.wait_recv()
-        return copies
-
-    started = exchange(0, term_ref, far)
+    z, q = cell // PLANE, lax.rem(cell, PLANE)
+    above = [lax.rem(z + d, 4) for d in range(1, 4)]
+    beside = [lax.rem(q + d, PLANE) for d in range(1, PLANE)]
+    columns = [{"cell": to * PLANE + q} for to in above]
+    plane = [{"cell": z * PLANE + to} for to in beside]
+    greet(columns + plane, len(columns) + len(plane))
+    started = []
+    for d, (to, device) in enumerate(zip(above, columns)):
+        started.append(remote(term_ref.at[to], far.at[d], far_s.at[d], far_r.at[d], device))
+        started[-1].start()
+    for copy in started:
+        copy.wait_recv()
     some = term_ref[z] + (far[0] + far[1] + far[2])
-    for q in range(4):
-        held_mid[q] = some[8 * q : 8 * q + 8]
-    started += exchange(1, held_mid, mid)
-    few = held_mid[y] + (mid[0] + mid[1] + mid[2])
-    for q in range(4):
-        held_near[q] = few[2 * q : 2 * q + 2]
-    started += exchange(2, held_near, near)
-    out_ref[...] = (held_near[x] + (near[0] + near[1] + near[2]))[:, :ORB]
-    for copy in started:
+    for k in range(PLANE):
+        held[k] = some[2 * k : 2 * k + 2]
+    wide = []
+    for d, (to, device) in enumerate(zip(beside, plane)):
+        wide.append(remote(held.at[to], near.at[d], near_s.at[d], near_r.at[d], device))
+        wide[-1].start()
+    for copy in wide:
+        copy.wait_recv()
+    out_ref[...] = (held[q] + jnp.sum(near[...], axis=0))[:, :ORB]
+    for copy in started + wide:
         copy.wait_send()
 
 
@@ -573,12 +569,12 @@
         out_specs=VMEM,
         scratch_shapes=[
             pltpu.VMEM((3, 32, 128), F32),
-            pltpu.VMEM((3, 8, 128), F32),
-            pltpu.VMEM((3, 2, 128), F32),
-            pltpu.VMEM((4, 8, 128), F32),
-            pltpu.VMEM((4, 2, 128), F32),
-            pltpu.SemaphoreType.DMA((3, 3)),
-            pltpu.SemaphoreType.DMA((3, 3)),
+            pltpu.VMEM((PLANE - 1, 2, 128), F32),
+            pltpu.VMEM((PLANE, 2, 128), F32),
+            pltpu.SemaphoreType.DMA((3,)),
+            pltpu.SemaphoreType.DMA((3,)),
+            pltpu.SemaphoreType.DMA((PLANE - 1,)),
+            pltpu.SemaphoreType.DMA((PLANE - 1,)),
         ],
         compiler_params=pltpu.CompilerParams(collective_id=2, has_side_effects=True, vmem_limit_bytes=VMEM_LIMIT),
     )(terms)

time: 92.3 us -> 91.9 us (level)
  no operation moved by 1% of the time
where the time goes in v4:
time: 91.9 us; the launch traced here: 91.6 us
  Pallas kernels  86.8 us (94%)
  local copies, waits for them, and re-layouts  2.04 us (2%)
  starting transfers between devices  2 us (2%)
    pallas_call x1, Pallas kernels, total(): pl.pallas_call(total_kernel, out_shape=jax.ShapeDtypeStruct((2, ORB), F32...  31.6 us
    pallas_call x1, Pallas kernels, elements(): pl.pallas_call(element_kernel, out_shape=(jax.ShapeDtypeStruct((PACKED, 1...  24.2 us
    pallas_call x1, Pallas kernels, collect(): pl.pallas_call(collect_kernel, out_shape=jax.ShapeDtypeStruct((LOCAL, 2 *...  13.1 us
    pallas_call x1, Pallas kernels, swap(): pl.pallas_call(swap_kernel, out_shape=(jax.ShapeDtypeStruct((LOW, 128), B...  9.65 us
    pallas_call x1, Pallas kernels, finish(): pl.pallas_call(finish_kernel, out_shape=(jax.ShapeDtypeStruct((ORB, OWN),...  8.29 us
    ppermute x1, starting transfers between devices, shards(): far = lax.ppermute(panels, 'orb', [(0, 2), (2, 0), (1, 3), (3, 1)])  2 us
  transfers between devices with their start and end apart: 1, of which 0 were waited for; matrix products, arithmetic and copies ran while one was open for 1% of the time, Pallas kernels for 26%

profile of v4, /device:TPU:2, one launch (start us, length us, event | category | flops | bytes accessed | tf_op | source)
XLA Modules:
  0.0 91.6 jit_solution(17086511959603011179)
XLA Ops:
  0.6 0.0 copy-start
  0.6 0.0 copy-start.1
  0.7 13.1 %shard_map.77.table_ref = f32[12096,128]{1,0:T(8,128)} custom-call(bf16[64,10368]{1,0:T(8,128)(2,1)} %orb_ref.1, s32[1728]{0:T(1024)} %bound_ref.3), custom_call_target="tpu_custom_call" | custom-call | tf_op jit(solution)/shard_map/pallas_call | solution.py:174
  13.8 0.0 copy-done
  13.8 2.0 %collective-permute-start = (bf16[32,10368]{1,0:T(8,128)(2,1)S(1)}, bf16[32,10368]{1,0:T(8,128)(2,1)}, u32[]{:S(2)}, u32[]{:S(2)}) collective-permute-start(bf16[32,10368]{1,0:T(8,128)(2,1)S(1)} %copy-done), channel_id=1, source_target_pairs={{0,2},{2,0},{1,3},{3,1},{4,6},{6,4},{5,7},{7,5},{8,10},{10,8},{9,1... | collective-permute-start | bytes 1990664 | tf_op jit(solution)/shard_map/ppermute | solution.py:586
  15.8 0.0 copy-done.1
  15.8 0.8 reshape.10.conn_hbm
  16.6 24.2 %shard_map.78 = (f32[6112,128]{1,0:T(8,128)}, bf16[6112,128]{1,0:T(8,128)(2,1)}) custom-call(s32[16464]{0:T(1024)} %reshape.10.conn_hbm, s32[48,343]{1,0:T(8,128)} %bitcast.3, f32[48,343]{1,0:T(8,128)} %bitcast.5, bf16[343,343]{1,0:T(8,128)(2,1)} %stiff_ref.1, f32[12096,128]{1,0:T(8,128)} %shard_map.77.table_ref), custom_call_target="tpu_custom_call" | custom-call | flops 722835456 | bytes 62914560 | tf_op jit(solution)/shard_map/pallas_call | solution.py:332
  40.8 0.0 collective-permute-done.far_ref
  40.8 9.6 %shard_map.79 = (bf16[5248,128]{1,0:T(8,128)(2,1)}, bf16[864,128]{1,0:T(8,128)(2,1)}, bf16[64,10368]{1,0:T(8,128)(2,1)}) custom-call(f32[6112,128]{1,0:T(8,128)} %get-tuple-element.12.own_ref, bf16[6112,128]{1,0:T(8,128)(2,1)} %get-tuple-element.13.leave_ref, bf16[32,10368]{1,0:T(8,128)(2,1)} %mine_ref, bf16[32,10368]{1,0:T(8,128)(2,1)} %collective-permute-done.far_ref), custom_call_target="tpu_custom_call" | custom-call | tf_op jit(solution)/shard_map/pallas_call | solution.py:412
  50.5 8.3 %shard_map.80 = (bf16[64,10368]{1,0:T(8,128)(2,1)}, f32[128,128]{1,0:T(8,128)}) custom-call(s32[1728]{0:T(1024)} %bound_ref.3, f32[6112,128]{1,0:T(8,128)} %get-tuple-element.12.own_ref, bf16[5248,128]{1,0:T(8,128)(2,1)} %get-tuple-element.15.got_ref, bf16[864,128]{1,0:T(8,128)(2,1)} %get-tuple-element.16.in_ref, bf16[32,10368]{1,0:T(8,128)(2,1)} %mine_ref, ...), custom_call_target="tpu_custom_call" | custom-call | tf_op jit(solution)/shard_map/pallas_call | solution.py:514
  58.7 31.6 %shard_map.81 = f32[2,64]{1,0:T(2,128)} custom-call(f32[4,32,128]{2,1,0:T(8,128)} %bitcast.6), custom_call_target="tpu_custom_call" | custom-call | tf_op jit(solution)/shard_map/pallas_call | solution.py:565
  90.4 1.2 %copy.9 = f32[2,64]{1,0:T(2,128)} copy(f32[2,64]{1,0:T(2,128)} %shard_map.81) | data formatting | bytes 1024
Async XLA Ops:
  0.6 13.1 %copy-start = (bf16[32,10368]{1,0:T(8,128)(2,1)S(1)}, bf16[32,10368]{1,0:T(8,128)(2,1)}, u32[]{:S(2)}) copy-start(bf16[32,10368]{1,0:T(8,128)(2,1)} %mine_ref) | copy-start | bytes 1990660
  0.6 15.1 %copy-start.1 = (s32[343,48]{0,1:T(8,128)S(1)}, s32[343,48]{0,1:T(8,128)}, u32[]{:S(2)}) copy-start(s32[343,48]{0,1:T(8,128)} %param.10) | copy-start | bytes 197572
  13.8 27.0 %collective-permute-start = (bf16[32,10368]{1,0:T(8,128)(2,1)S(1)}, bf16[32,10368]{1,0:T(8,128)(2,1)}, u32[]{:S(2)}, u32[]{:S(2)}) collective-permute-start(bf16[32,10368]{1,0:T(8,128)(2,1)S(1)} %copy-done), channel_id=1, source_target_pairs={{0,2},{2,0},{1,3},{3,1},{4,6},{6,4},{5,7},{7,5},{8,10},{10,8},{9,1... | collective-permute-start | bytes 1990664 | tf_op jit(solution)/shard_map/ppermute | solution.py:586
